TPU v7x, 32 devices: a whole 2x2x4 slice. The times are simulated.
32 devices in a mesh: group: 2 (over y), ctx: 16 (over z, x, core).
Axes of the slice: x: 2, y: 2, z: 4, core: 2. Of those that a mesh axis runs over, the one named last changes fastest.
Arguments:
- queries: bfloat16 [8192, 3072], P(('group', 'ctx')), parts along dimension 0, may hold values from -200 to 200
- key_matrix: bfloat16 [8192, 512], P(('group', 'ctx')), parts along dimension 0, may hold values from -4 to 4
- value_matrix: bfloat16 [8192, 512], P(('group', 'ctx')), parts along dimension 0, may hold values from -6 to 6
- tile_lists: int32 [64, 6], P(('group', 'ctx')), parts along dimension 0, may hold values from -1 to 31, as said below
- moe_tokens: bfloat16 [512, 3072], P(('group', 'ctx')), parts along dimension 0, may hold values from -6 to 6
- expert_ids: int32 [512, 2], P(('group', 'ctx')), parts along dimension 0, may hold values from 0 to 7, all different within a row; in each aligned block of 16 rows (0 to 15, 16 to 31, ...) at most 5 rows name the same one
- router_weight: bfloat16 [3072, 8], replicated, may hold values from -0.109375 to 0.109375
- gate_weight: bfloat16 [3072, 65536], P(None, 'ctx'), may hold values from -0.109375 to 0.109375
- up_weight: bfloat16 [3072, 65536], P(None, 'ctx'), may hold values from -0.109375 to 0.109375
- down_weight: bfloat16 [65536, 3072], P('ctx'), may hold values from -0.0625 to 0.0625
Outputs:
- attended: bfloat16 [8192, 3072], P(('group', 'ctx')), parts along dimension 0
- combined: bfloat16 [512, 3072], P(('group', 'ctx')), parts along dimension 0
There are 2 independent parts, one for each index of `group`. A program takes and returns all parts, laid end to end along the dimension named above; an argument that names none is the same for every part. Nothing has to cross between parts.
Inputs may be any that keep to these rules, and one draw needn't show every extreme that they name: `tile_lists`: entry 0 of row b is b itself; the next entries are distinct key tiles before b whose positions lie on the same device as tile b or on one of the 4 devices before it; the rest of the row is -1. Some row lists 6 tiles. `expert_ids`: each token picks two different experts; among the 16 tokens of one device no expert is picked more than 5 times.
All inputs are finite; a program needn't handle non-finite values.
Results may differ from a plain program's by a relative error of at most 0.0049.
Values may be sent and summed in bfloat16 or wider, within the bound.
No kernel may reach another device: no remote copies, remote signals or barrier semaphores. Data moves between devices by JAX's collectives and lax.ppermute only.
A program may use at most 192 MiB of HBM per device.

v0:
```python
import functools

import jax
import jax.numpy as jnp
from jax import lax
from jax.experimental import pallas as pl
from jax.experimental.pallas import tpu as pltpu
from jax.sharding import PartitionSpec as P

TILE_POSITIONS = 128
HEAD_SIZE = 128
KEY_VALUE_HEADS = 4
QUERY_HEADS = 24
QUERY_PER_GROUP = 6
PRIOR_DEVICES = 4
MOST_LISTED = 6
D = 3072
EXPERTS = 8
TOP = 2
CAP = 5

PARTS = 24
PART_WIDTH = D // PARTS
PIECES = 4
FIRST_HELD = D // 4
HIDDEN_CHUNK = 512
HEADS_PER_STEP = 2
LOG2_E = 1.4426950408889634
MIB = 2**20

WINDOW_SOURCES = ((2, 5, 1, 4, 0), (2, 4, 1, 3, 0))


def in_vmem(x):
    return pltpu.with_memory_space_constraint(x, pltpu.VMEM)


def in_hbm(x):
    return pltpu.with_memory_space_constraint(x, pltpu.HBM)


def exchanged(x, by):
    devices = lax.axis_size("ctx")
    return lax.ppermute(x, "ctx", [(i, i ^ by) for i in range(devices)])


def passed_along(x, by):
    devices = lax.axis_size("ctx")
    return lax.ppermute(x, "ctx", [(i, (i + by) % devices) for i in range(devices)])


def same_core_exchange(x):
    devices = lax.axis_size("ctx")
    groups = [[core + 2 * i for i in range(devices // 2)] for core in range(2)]
    return lax.all_to_all(x, "ctx", split_axis=0, concat_axis=0, tiled=True, axis_index_groups=groups)


def pack_kernel(ids_ref, base_ref, tokens_ref, keep_ref, send_ref, rows_ref, slots_ref, count_ref):
    tokens = tokens_ref.shape[0]
    base = base_ref[0]
    for part in range(PARTS):
        columns = slice(part * PART_WIDTH, (part + 1) * PART_WIDTH)
        rows_ref[pl.ds(part, tokens, stride=PARTS), :] = tokens_ref[:, columns].astype(jnp.float32)
    slots_ref[...] = jnp.zeros_like(slots_ref)
    for expert in range(EXPERTS):
        count_ref[expert] = 0
    for token in range(tokens):
        row = rows_ref[token * PARTS : (token + 1) * PARTS, :].astype(jnp.bfloat16)
        for pick in range(TOP):
            expert = ids_ref[pick, token]
            slot = count_ref[expert]
            count_ref[expert] = slot + 1
            place = lax.bitwise_xor(expert, base)
            slots_ref[lax.bitwise_and(place, 1), lax.shift_right_logical(place, 1), slot] = row
    keep_ref[...] = slots_ref[0]
    send_ref[...] = slots_ref[1]


def pack(ids, base, moe_tokens):
    tokens = moe_tokens.shape[0]
    smem = pl.BlockSpec(memory_space=pltpu.SMEM)
    vmem = pl.BlockSpec(memory_space=pltpu.VMEM)
    half = (EXPERTS // 2, CAP, PARTS, PART_WIDTH)
    return pl.pallas_call(
        pack_kernel,
        out_shape=(jax.ShapeDtypeStruct(half, jnp.bfloat16),) * 2,
        in_specs=[smem, smem, vmem],
        out_specs=(vmem, vmem),
        scratch_shapes=[
            pltpu.VMEM((tokens * PARTS, PART_WIDTH), jnp.float32),
            pltpu.VMEM((2,) + half, jnp.bfloat16),
            pltpu.SMEM((EXPERTS,), jnp.int32),
        ],
        compiler_params=pltpu.CompilerParams(vmem_limit_bytes=4 * MIB),
        name="pack",
    )(in_hbm(ids), base, in_hbm(moe_tokens))


def join_kernel(keep_ref, came_ref, mark_ref, *out_refs):
    for place, ref in enumerate(out_refs[:-1]):
        ref[0] = keep_ref[place]
        ref[1] = came_ref[place]
    out_refs[-1][...] = mark_ref[...] + 1


def join(keep, came, mark):
    vmem = pl.BlockSpec(memory_space=pltpu.VMEM)
    shape = jax.ShapeDtypeStruct((2,) + keep.shape[1:], keep.dtype)
    count = keep.shape[0]
    return pl.pallas_call(
        join_kernel,
        out_shape=(shape,) * count + (jax.ShapeDtypeStruct(mark.shape, mark.dtype),),
        in_specs=[vmem] * 3,
        out_specs=(vmem,) * (count + 1),
        compiler_params=pltpu.CompilerParams(vmem_limit_bytes=4 * MIB),
        name="join",
    )(keep, came, mark)


def merge_kernel(mark_ref, *refs):
    for place, ref in enumerate(refs[:-1]):
        refs[-1][2 * place : 2 * place + 2] = ref[...]


def merge(mark, pieces):
    vmem = pl.BlockSpec(memory_space=pltpu.VMEM)
    return pl.pallas_call(
        merge_kernel,
        out_shape=jax.ShapeDtypeStruct((2 * len(pieces),) + pieces[0].shape[1:], pieces[0].dtype),
        in_specs=[vmem] * (1 + len(pieces)),
        out_specs=vmem,
        compiler_params=pltpu.CompilerParams(vmem_limit_bytes=4 * MIB),
        name="merge",
    )(mark, *pieces)


def hold_kernel(first, mark_ref, gate_ref, next_ref, held_ref, sems):
    rows = held_ref.shape[0] // PIECES
    copies = [
        pltpu.make_async_copy(
            gate_ref.at[pl.ds(first + piece * rows, rows)], held_ref.at[pl.ds(piece * rows, rows)], sems.at[piece]
        )
        for piece in range(PIECES)
    ]
    for copy in copies:
        copy.start()
    next_ref[...] = mark_ref[...] + 1
    for copy in copies:
        copy.wait()


def hold(mark, gate_weight, first, count):
    vmem = pl.BlockSpec(memory_space=pltpu.VMEM)
    anywhere = pl.BlockSpec(memory_space=pl.ANY)
    columns = gate_weight.shape[1]
    return pl.pallas_call(
        functools.partial(hold_kernel, first),
        out_shape=(jax.ShapeDtypeStruct(mark.shape, mark.dtype), pltpu.VMEM((count, columns), gate_weight.dtype)),
        in_specs=[vmem, anywhere],
        out_specs=(vmem, vmem),
        scratch_shapes=[pltpu.SemaphoreType.DMA((PIECES,))],
        compiler_params=pltpu.CompilerParams(vmem_limit_bytes=MIB),
        cost_estimate=pl.CostEstimate(flops=10**6, bytes_accessed=2 * count * columns, transcendentals=0),
        name="hold",
    )(mark, in_hbm(gate_weight))


def shares_of(ids_ref, tokens_ref, router_ref):
    logits = lax.dot_general(
        router_ref[...], tokens_ref[...], (((1,), (1,)), ((), ())), preferred_element_type=jnp.float32
    )
    places = lax.broadcasted_iota(jnp.int32, logits.shape, 0)
    ids = ids_ref[...]
    picked = [
        jnp.sum(jnp.where(places == ids[pick : pick + 1, :], logits, 0.0), axis=0, keepdims=True)
        for pick in range(TOP)
    ]
    top = jnp.maximum(picked[0], picked[1])
    weights = [jnp.exp(value - top) for value in picked]
    total = weights[0] + weights[1]
    return jnp.concatenate([weights[0] / total, weights[1] / total], axis=0)


def prepare_kernel(
    first, mark_ref, ids_ref, tokens_ref, router_ref, gate_ref, key_ref, value_ref,
    next_ref, shares_ref, pair_ref, held_ref, tokens_vmem, router_vmem, sems, pair_sems,
):
    rows = held_ref.shape[0] // PIECES
    copies = [
        pltpu.make_async_copy(ref, pair_ref.at[place], pair_sems.at[place])
        for place, ref in enumerate((key_ref, value_ref))
    ]
    copies += [
        pltpu.make_async_copy(
            gate_ref.at[pl.ds(first + piece * rows, rows)], held_ref.at[pl.ds(piece * rows, rows)], sems.at[piece]
        )
        for piece in range(PIECES)
    ]
    small = [
        pltpu.make_async_copy(tokens_ref, tokens_vmem, pair_sems.at[2]),
        pltpu.make_async_copy(router_ref, router_vmem, pair_sems.at[3]),
    ]
    for copy in small + copies:
        copy.start()
    next_ref[...] = mark_ref[...] + 1
    for copy in small:
        copy.wait()
    shares_ref[...] = shares_of(ids_ref, tokens_vmem, router_vmem)
    for copy in copies:
        copy.wait()


def prepare(mark, ids, moe_tokens, router_weight, gate_weight, keys, values, first, count):
    vmem = pl.BlockSpec(memory_space=pltpu.VMEM)
    anywhere = pl.BlockSpec(memory_space=pl.ANY)
    columns = gate_weight.shape[1]
    return pl.pallas_call(
        functools.partial(prepare_kernel, first),
        out_shape=(
            jax.ShapeDtypeStruct(mark.shape, mark.dtype),
            jax.ShapeDtypeStruct(ids.shape, jnp.float32),
            jax.ShapeDtypeStruct((2,) + keys.shape, keys.dtype),
            pltpu.VMEM((count, columns), gate_weight.dtype),
        ),
        in_specs=[vmem] * 2 + [anywhere] * 5,
        out_specs=(vmem, vmem, anywhere, vmem),
        scratch_shapes=[
            pltpu.VMEM(moe_tokens.shape, moe_tokens.dtype),
            pltpu.VMEM(router_weight.shape[::-1], router_weight.dtype),
            pltpu.SemaphoreType.DMA((PIECES,)),
            pltpu.SemaphoreType.DMA((4,)),
        ],
        compiler_params=pltpu.CompilerParams(vmem_limit_bytes=2 * MIB),
        cost_estimate=pl.CostEstimate(flops=10**6, bytes_accessed=2 * count * columns, transcendentals=0),
        name="prepare",
    )(mark, *map(in_hbm, (ids, moe_tokens, router_weight.T, gate_weight, keys, values)))


def experts_kernel(helds, base_ref, near_ref, far_ref, *refs):
    gate_refs, refs = refs[:helds], refs[helds:]
    up_ref, down_ref, mine_ref, other_ref, parts_ref, rows_ref, sums_ref, up_vmem, down_vmem, sems = refs
    senders = mine_ref.shape[0]
    count = 2 * senders * CAP
    chunks = up_ref.shape[1] // HIDDEN_CHUNK
    depth = down_vmem.shape[0]

    def span(chunk):
        return pl.ds(pl.multiple_of(chunk * HIDDEN_CHUNK, HIDDEN_CHUNK), HIDDEN_CHUNK)

    def up_copy(chunk, slot):
        return pltpu.make_async_copy(up_ref.at[:, span(chunk)], up_vmem.at[slot], sems.at[0, slot])

    def down_copy(chunk, slot):
        return pltpu.make_async_copy(down_ref.at[span(chunk)], down_vmem.at[slot], sems.at[1, slot])

    for chunk in range(min(depth, chunks)):
        up_copy(chunk, chunk).start()
        down_copy(chunk, chunk).start()
    for place, ref in enumerate((near_ref, far_ref)):
        here = ref.shape[0]

        def unpack(i, carry, place=place, ref=ref, here=here):
            first = pl.multiple_of((place * here + i) * CAP * PARTS, 8)
            parts_ref[pl.ds(first, CAP * PARTS), :] = (
                ref[i].astype(jnp.float32).reshape(CAP * PARTS, PART_WIDTH)
            )
            return carry

        lax.fori_loop(0, here, unpack, 0)
    for part in range(PARTS):
        columns = slice(part * PART_WIDTH, (part + 1) * PART_WIDTH)
        rows_ref[:, columns] = parts_ref[pl.ds(part, count, stride=PARTS), :].astype(jnp.bfloat16)

    def work(chunk, first):
        slot = lax.rem(chunk, depth)
        gate_value, first_row = None, 0
        for ref in gate_refs:
            part = jnp.dot(
                rows_ref[:, first_row : first_row + ref.shape[0]], ref[:, span(chunk)], preferred_element_type=jnp.float32
            )
            gate_value = part if gate_value is None else gate_value + part
            first_row += ref.shape[0]
        up_copy(chunk, slot).wait()
        up_value = jnp.dot(rows_ref[...], up_vmem[slot], preferred_element_type=jnp.float32)
        hidden = (gate_value / (1.0 + jnp.exp(-gate_value)) * up_value).astype(jnp.bfloat16)

        @pl.when(chunk + depth < chunks)
        def _():
            up_copy(chunk + depth, slot).start()

        down_copy(chunk, slot).wait()
        product = jnp.dot(hidden, down_vmem[slot], preferred_element_type=jnp.float32)
        if first:
            sums_ref[...] = product
        else:
            sums_ref[...] += product

        @pl.when(chunk + depth < chunks)
        def _():
            down_copy(chunk + depth, slot).start()

    work(jnp.int32(0), True)

    def step(chunk, carry):
        work(chunk, False)
        return carry

    lax.fori_loop(1, chunks, step, 0)
    for part in range(PARTS):
        columns = slice(part * PART_WIDTH, (part + 1) * PART_WIDTH)
        parts_ref[pl.ds(part, count, stride=PARTS), :] = sums_ref[:, columns]

    def give(i, carry):
        first = pl.multiple_of(i * CAP * PARTS, 8)
        sender = lax.bitwise_xor(jnp.int32(i), base_ref[0])
        mine_ref[sender] = parts_ref[pl.ds(first, CAP * PARTS), :].reshape(CAP, PARTS, PART_WIDTH)
        second = pl.multiple_of((senders + i) * CAP * PARTS, 8)
        other_ref[sender] = (
            parts_ref[pl.ds(second, CAP * PARTS), :].reshape(CAP, PARTS, PART_WIDTH).astype(jnp.bfloat16)
        )
        return carry

    lax.fori_loop(0, senders, give, 0)


def experts(base, near, far, gate_held, up_weight, down_weight):
    shape = near.shape
    count = 2 * shape[0] * CAP
    smem = pl.BlockSpec(memory_space=pltpu.SMEM)
    vmem = pl.BlockSpec(memory_space=pltpu.VMEM)
    anywhere = pl.BlockSpec(memory_space=pl.ANY)
    depth = min(3, up_weight.shape[1] // HIDDEN_CHUNK)
    return pl.pallas_call(
        functools.partial(experts_kernel, len(gate_held)),
        out_shape=(jax.ShapeDtypeStruct(shape, jnp.float32), jax.ShapeDtypeStruct(shape, jnp.bfloat16)),
        in_specs=[smem] + [vmem] * (2 + len(gate_held)) + [anywhere, anywhere],
        out_specs=(vmem, vmem),
        scratch_shapes=[
            pltpu.VMEM((count * PARTS, PART_WIDTH), jnp.float32),
            pltpu.VMEM((count, D), jnp.bfloat16),
            pltpu.VMEM((count, D), jnp.float32),
            pltpu.VMEM((depth, D, HIDDEN_CHUNK), jnp.bfloat16),
            pltpu.VMEM((depth, HIDDEN_CHUNK, D), jnp.bfloat16),
            pltpu.SemaphoreType.DMA((2, depth)),
        ],
        compiler_params=pltpu.CompilerParams(vmem_limit_bytes=32 * MIB),
        cost_estimate=pl.CostEstimate(
            flops=6 * count * up_weight.size, bytes_accessed=6 * up_weight.size, transcendentals=0
        ),
        name="experts",
    )(
        base,
        in_vmem(near),
        in_vmem(far),
        *map(in_vmem, gate_held),
        in_hbm(up_weight),
        in_hbm(down_weight),
    )


def add_kernel(mine_ref, other_ref, sum_ref, mark_ref):
    sum_ref[...] = (mine_ref[...] + other_ref[...].astype(jnp.float32)).astype(jnp.bfloat16)
    mark_ref[...] = jnp.zeros_like(mark_ref)


def add(mine, other):
    vmem = pl.BlockSpec(memory_space=pltpu.VMEM)
    return pl.pallas_call(
        add_kernel,
        out_shape=(jax.ShapeDtypeStruct(mine.shape, jnp.bfloat16), jax.ShapeDtypeStruct((8, 128), jnp.float32)),
        in_specs=[vmem, vmem],
        out_specs=(vmem, vmem),
        compiler_params=pltpu.CompilerParams(vmem_limit_bytes=24 * MIB),
        name="add",
    )(mine, other)


def follow_kernel(mark_ref, *refs):
    del mark_ref, refs


def follow(mark, arrays):
    anywhere = pl.BlockSpec(memory_space=pl.ANY)
    return pl.pallas_call(
        follow_kernel,
        out_shape=tuple(jax.ShapeDtypeStruct(x.shape, x.dtype) for x in arrays),
        in_specs=[anywhere] * (1 + len(arrays)),
        out_specs=(anywhere,) * len(arrays),
        input_output_aliases={1 + i: i for i in range(len(arrays))},
        compiler_params=pltpu.CompilerParams(vmem_limit_bytes=MIB),
        name="follow",
    )(mark, *arrays)


def combine_kernel(ids_ref, shares_ref, back_ref, out_ref, rows_ref, count_ref):
    tokens = out_ref.shape[0]
    holders = back_ref.shape[0] // EXPERTS
    for expert in range(EXPERTS):
        count_ref[expert] = 0
    for token in range(tokens):
        total = None
        for pick in range(TOP):
            expert = ids_ref[pick, token]
            slot = count_ref[expert]
            count_ref[expert] = slot + 1
            value = back_ref[expert * holders, slot].astype(jnp.float32)
            for holder in range(1, holders):
                value += back_ref[expert * holders + holder, slot].astype(jnp.float32)
            value = shares_ref[pick, token] * value
            total = value if total is None else total + value
        rows_ref[token * PARTS : (token + 1) * PARTS, :] = total
    for part in range(PARTS):
        columns = slice(part * PART_WIDTH, (part + 1) * PART_WIDTH)
        out_ref[:, columns] = rows_ref[pl.ds(part, tokens, stride=PARTS), :].astype(jnp.bfloat16)


def combine(ids, gate_shares, back):
    tokens = ids.shape[1]
    smem = pl.BlockSpec(memory_space=pltpu.SMEM)
    vmem = pl.BlockSpec(memory_space=pltpu.VMEM)
    return pl.pallas_call(
        combine_kernel,
        out_shape=jax.ShapeDtypeStruct((tokens, D), jnp.bfloat16),
        in_specs=[smem, smem, vmem],
        out_specs=vmem,
        scratch_shapes=[
            pltpu.VMEM((tokens * PARTS, PART_WIDTH), jnp.float32),
            pltpu.SMEM((EXPERTS,), jnp.int32),
        ],
        compiler_params=pltpu.CompilerParams(vmem_limit_bytes=16 * MIB),
        name="combine",
    )(in_hbm(ids), gate_shares, back)


def attention_kernel(
    place_ref, lists_ref, query_ref, b0, b1, b2, b3, b4, b5, out_ref, window, scores, weights, sems
):
    tile, step = pl.program_id(0), pl.program_id(1)
    copies = [
        pltpu.make_async_copy(ref, window.at[i], sems.at[i]) for i, ref in enumerate((b0, b1, b2, b3, b4, b5))
    ]

    @pl.when((tile == 0) & (step == 0))
    def _():
        for copy in copies:
            copy.start()
        for copy in copies:
            copy.wait()

    tiles_here = b0.shape[1] // TILE_POSITIONS
    first_tile = place_ref[0]
    listed_count = jnp.int32(1)
    for entry in range(1, MOST_LISTED):
        listed_count += (lists_ref[tile, entry] >= 0).astype(jnp.int32)

    def fetch(which, entry, head):
        relative = jnp.clip(lists_ref[tile, entry] - first_tile, 0, (PRIOR_DEVICES + 1) * tiles_here - 1)
        source = place_ref[1 + lax.div(relative, tiles_here)]
        first = pl.multiple_of(lax.rem(relative, tiles_here) * TILE_POSITIONS, TILE_POSITIONS)
        columns = pl.ds(pl.multiple_of((step * HEADS_PER_STEP + head) * HEAD_SIZE, HEAD_SIZE), HEAD_SIZE)
        return window[source, which, pl.ds(first, TILE_POSITIONS), columns]

    def attend(listed):
        width = listed * TILE_POSITIONS
        units = [(head, part) for head in range(HEADS_PER_STEP) for part in range(2)]
        group_count = QUERY_PER_GROUP // 2
        row_place = lax.broadcasted_iota(jnp.int32, (TILE_POSITIONS, TILE_POSITIONS), 0)
        column_place = lax.broadcasted_iota(jnp.int32, (TILE_POSITIONS, TILE_POSITIONS), 1)
        causal = column_place <= row_place
        totals = {}

        def columns_of(unit, group):
            head, part = units[unit]
            first = (head * QUERY_PER_GROUP + part * group_count + group) * HEAD_SIZE
            return slice(first, first + HEAD_SIZE)

        def score(unit):
            head = units[unit][0]
            rows = jnp.concatenate([query_ref[:, columns_of(unit, group)] for group in range(group_count)], axis=0)
            keys = jnp.concatenate([fetch(0, entry, head) for entry in range(listed)], axis=0)
            scores[unit, :, :width] = lax.dot_general(
                rows, keys, (((1,), (1,)), ((), ())), preferred_element_type=jnp.float32
            )

        def weigh(unit):
            for group in range(group_count):
                rows = slice(group * TILE_POSITIONS, (group + 1) * TILE_POSITIONS)
                blocks = [jnp.where(causal, scores[unit, rows, :TILE_POSITIONS], -1e30)]
                blocks += [
                    scores[unit, rows, entry * TILE_POSITIONS : (entry + 1) * TILE_POSITIONS]
                    for entry in range(1, listed)
                ]
                top = blocks[0]
                for block in blocks[1:]:
                    top = jnp.maximum(top, block)
                top = jnp.max(top, axis=1, keepdims=True)
                total = None
                for entry, block in enumerate(blocks):
                    weight = jnp.exp2((block - top) * (HEAD_SIZE**-0.5 * LOG2_E))
                    total = weight if total is None else total + weight
                    weights[unit, rows, entry * TILE_POSITIONS : (entry + 1) * TILE_POSITIONS] = weight.astype(
                        jnp.bfloat16
                    )
                totals[unit, group] = jnp.sum(total, axis=1, keepdims=True)

        def finish(unit):
            head = units[unit][0]
            values = jnp.concatenate([fetch(1, entry, head) for entry in range(listed)], axis=0)
            summed = jnp.dot(weights[unit, :, :width], values, preferred_element_type=jnp.float32)
            for group in range(group_count):
                rows = slice(group * TILE_POSITIONS, (group + 1) * TILE_POSITIONS)
                out_ref[:, columns_of(unit, group)] = (summed[rows] / totals[unit, group]).astype(jnp.bfloat16)

        for turn in range(len(units) + 2):
            if turn < len(units):
                score(turn)
            if 0 <= turn - 2:
                finish(turn - 2)
            if 0 <= turn - 1 < len(units):
                weigh(turn - 1)

    for listed in range(1, MOST_LISTED + 1):
        pl.when(listed_count == listed)(functools.partial(attend, listed))


def attention(place, tile_lists, queries, blocks):
    rows_here = queries.shape[0]
    tiles_here = rows_here // TILE_POSITIONS
    group_width = HEADS_PER_STEP * QUERY_PER_GROUP * HEAD_SIZE
    anywhere = pl.BlockSpec(memory_space=pl.ANY)
    query_spec = pl.BlockSpec((TILE_POSITIONS, group_width), lambda tile, step, *_: (tile, step))
    unit = (2 * HEADS_PER_STEP, QUERY_PER_GROUP // 2 * TILE_POSITIONS, MOST_LISTED * TILE_POSITIONS)
    most = MOST_LISTED * TILE_POSITIONS
    return pl.pallas_call(
        attention_kernel,
        out_shape=jax.ShapeDtypeStruct(queries.shape, jnp.bfloat16),
        grid_spec=pltpu.PrefetchScalarGridSpec(
            num_scalar_prefetch=2,
            grid=(tiles_here, KEY_VALUE_HEADS // HEADS_PER_STEP),
            in_specs=[query_spec] + [anywhere] * 6,
            out_specs=query_spec,
            scratch_shapes=[
                pltpu.VMEM((6, 2, rows_here, KEY_VALUE_HEADS * HEAD_SIZE), jnp.bfloat16),
                pltpu.VMEM(unit, jnp.float32),
                pltpu.VMEM(unit, jnp.bfloat16),
                pltpu.SemaphoreType.DMA((6,)),
            ],
        ),
        compiler_params=pltpu.CompilerParams(vmem_limit_bytes=24 * MIB),
        cost_estimate=pl.CostEstimate(
            flops=4 * most * queries.size, bytes_accessed=8 * queries.size, transcendentals=most * queries.size // 128
        ),
        name="attention",
    )(place, tile_lists, in_hbm(queries), *blocks)


def shards(
    queries,
    key_matrix,
    value_matrix,
    tile_lists,
    moe_tokens,
    expert_ids,
    router_weight,
    gate_weight,
    up_weight,
    down_weight,
):
    devices = lax.axis_size("ctx")
    me = lax.axis_index("ctx")
    ids = expert_ids.T
    direct = devices == 2 * EXPERTS
    base = (me // 2 if direct else jnp.zeros_like(me)).astype(jnp.int32)[None]
    keep, send = pack(ids, base, moe_tokens)
    mark = jnp.zeros((8, 128), jnp.float32)
    rest = (ids, moe_tokens, router_weight, gate_weight, key_matrix, value_matrix)
    if direct:
        came = exchanged(send, 2)
        mark, first_held = hold(mark, gate_weight, 0, FIRST_HELD)
        *pieces, mark = join(keep, came, mark)
        pieces[1:] = [exchanged(pieces[place], 4 * place) for place in range(1, len(pieces))]
        mark, gate_shares, own, second_held = prepare(mark, *rest, FIRST_HELD, D - FIRST_HELD)
        near = merge(mark, pieces)
        gate_held = [first_held, second_held]
    else:
        packed = jnp.stack([keep, send], axis=1).reshape((EXPERTS,) + keep.shape[1:])
        near = same_core_exchange(jnp.repeat(packed, devices // (2 * EXPERTS), axis=0))
        mark, gate_shares, own, held = prepare(mark, *rest, 0, D)
        gate_held = [held]
    far = exchanged(near, 1)
    two_before = passed_along(own, 2)
    four_before = passed_along(own, 4)
    mine, other = experts(base, near, far, gate_held, up_weight, down_weight)
    summed, mark = add(mine, exchanged(other, 1))
    back = same_core_exchange(summed)
    blocks = list(follow(mark, [own, two_before, four_before]))
    blocks += [exchanged(x, 1) for x in blocks]
    tiles_here = queries.shape[0] // TILE_POSITIONS
    sources = jnp.where(me % 2 == 0, *(jnp.array(row, jnp.int32) for row in WINDOW_SOURCES))
    place = jnp.concatenate([((me - PRIOR_DEVICES) * tiles_here).astype(jnp.int32)[None], sources])
    attended = attention(place, tile_lists, queries, blocks)
    attended, back = lax.optimization_barrier((attended, back))
    combined = combine(ids, gate_shares, back)
    return (attended, combined)


def solution(mesh):
    split = P(("group", "ctx"), None)
    placed = (split, split, split, split, split, split, P(), P(None, "ctx"), P(None, "ctx"), P("ctx", None))
    return jax.shard_map(shards, mesh=mesh, in_specs=placed, out_specs=(split, split), check_vma=False)
```

profile of v0, /device:TPU:9, one launch (start us, length us, event | category | flops | bytes accessed | tf_op | source)
XLA Modules:
  0.0 64.7 jit_solution(13953458876087936873)
XLA Ops:
  0.6 1.1 %pack.1 = (bf16[4,5,24,128]{3,2,1,0:T(8,128)(2,1)S(1)}, bf16[4,5,24,128]{3,2,1,0:T(8,128)(2,1)S(1)}) custom-call(s32[2,16]{1,0:T(2,128)} %bitcast.5, s32[1]{0:T(128)} %bitcast.1.base_ref, bf16[16,3072]{1,0:T(8,128)(2,1)} %tokens_ref.3), custom_call_target="tpu_custom_call" | custom-call | tf_op jit(solution)/shard_map/pack/pallas_call | solution.py:84
  1.8 1.3 %collective-permute-start = (bf16[4,5,24,128]{3,2,1,0:T(8,128)(2,1)S(1)}, bf16[4,5,24,128]{3,2,1,0:T(8,128)(2,1)S(1)}, u32[]{:S(2)}, u32[]{:S(2)}) collective-permute-start(bf16[4,5,24,128]{3,2,1,0:T(8,128)(2,1)S(1)} %get-tuple-element.25), channel_id=1, source_target_pairs={{0,2},{1,3},{2,0},{3,1},{4,6},{5,7},{6,4},{7,5},{8,10},{9,11},{10,... | collective-permute-start | bytes 368648 | tf_op jit(solution)/shard_map/ppermute | solution.py:44
  3.0 2.9 %hold.1 = (f32[8,128]{1,0:T(8,128)S(1)}, bf16[768,4096]{1,0:T(8,128)(2,1)S(1)}) custom-call(f32[8,128]{1,0:T(8,128)S(1)} %broadcast_in_dim.11.mark_ref, bf16[3072,4096]{1,0:T(8,128)(2,1)} %gate_ref.3), custom_call_target="tpu_custom_call" | custom-call | flops 1000000 | bytes 6291456 | tf_op jit(solution)/shard_map/hold/pallas_call | solution.py:156
  5.9 0.1 collective-permute-done.came_ref
  6.0 0.3 collective-permute-start.1
  6.3 2.2 %collective-permute-start.2 = (bf16[2,5,24,128]{3,2,1,0:T(8,128)(2,1)S(1)}, bf16[2,5,24,128]{3,2,1,0:T(8,128)(2,1)S(1)}, u32[]{:S(2)}, u32[]{:S(2)}) collective-permute-start(bf16[2,5,24,128]{3,2,1,0:T(8,128)(2,1)S(1)} %get-tuple-element.31), channel_id=1, source_target_pairs={{0,8},{1,9},{2,10},{3,11},{4,12},{5,13},{6,14},{7,15},{8,0},{9,1},... | collective-permute-start | bytes 184328 | tf_op jit(solution)/shard_map/ppermute | solution.py:44
  8.6 0.2 collective-permute-start.3
  8.8 7.4 %prepare.1 = (f32[8,128]{1,0:T(8,128)S(1)}, f32[2,16]{1,0:T(2,128)S(1)}, bf16[2,256,512]{2,1,0:T(8,128)(2,1)S(1)}, bf16[2304,4096]{1,0:T(8,128)(2,1)S(1)}) custom-call(f32[8,128]{1,0:T(8,128)S(1)} %get-tuple-element.27.mark_ref, s32[2,16]{1,0:T(2,128)} %bitcast.6, bf16[16,3072]{1,0:T(8,128)(2,1)} %tokens_ref.3, bf16[8,3072]{1,0:T(8,128)(2,1)} %bitcast.4, ...), custom_call_target="tpu_custom_call" | custom-call | flops 1000000 | bytes 18874368 | tf_op jit(solution)/shard_map/prepare/pallas_call | solution.py:217
  16.2 0.0 collective-permute-done.1.refs_1_
  16.2 0.0 collective-permute-done.2.refs_2_
  16.2 0.0 collective-permute-done.3.refs_3_
  16.2 2.5 %collective-permute-start.4 = (bf16[8,5,24,128]{3,2,1,0:T(8,128)(2,1)S(1)}, bf16[8,5,24,128]{3,2,1,0:T(8,128)(2,1)S(1)}, u32[]{:S(2)}, u32[]{:S(2)}) collective-permute-start(bf16[8,5,24,128]{3,2,1,0:T(8,128)(2,1)S(1)} %merge.1.near_ref), channel_id=1, source_target_pairs={{0,1},{1,0},{2,3},{3,2},{4,5},{5,4},{6,7},{7,6},{8,9},{9,8},{10,11... | collective-permute-start | bytes 737288 | tf_op jit(solution)/shard_map/ppermute | solution.py:44
  18.7 1.3 %collective-permute-start.7 = (bf16[2,256,512]{2,1,0:T(8,128)(2,1)S(1)}, bf16[2,256,512]{2,1,0:T(8,128)(2,1)S(1)}, u32[]{:S(2)}, u32[]{:S(2)}) collective-permute-start(bf16[2,256,512]{2,1,0:T(8,128)(2,1)S(1)} %get-tuple-element.38.refs_0_), channel_id=1, source_target_pairs={{0,4},{1,5},{2,6},{3,7},{4,8},{5,9},{6,10},{7,11},{8,12},{9,13},{1... | collective-permute-start | bytes 1572872 | tf_op jit(solution)/shard_map/ppermute | solution.py:49
  20.0 1.2 %collective-permute-start.6 = (bf16[2,256,512]{2,1,0:T(8,128)(2,1)S(1)}, bf16[2,256,512]{2,1,0:T(8,128)(2,1)S(1)}, u32[]{:S(2)}, u32[]{:S(2)}) collective-permute-start(bf16[2,256,512]{2,1,0:T(8,128)(2,1)S(1)} %get-tuple-element.38.refs_0_), channel_id=1, source_target_pairs={{0,2},{1,3},{2,4},{3,5},{4,6},{5,7},{6,8},{7,9},{8,10},{9,11},{10,... | collective-permute-start | bytes 1572872 | tf_op jit(solution)/shard_map/ppermute | solution.py:49
  21.2 0.0 collective-permute-done.4.far_ref
  21.2 0.0 copy-start.2
  21.2 0.0 copy-start.3
  21.2 0.0 copy-start.1
  21.2 18.9 %experts.1 = (f32[8,5,24,128]{3,2,1,0:T(8,128)}, bf16[8,5,24,128]{3,2,1,0:T(8,128)(2,1)}) custom-call(s32[1]{0:T(128)} %bitcast.1.base_ref, bf16[8,5,24,128]{3,2,1,0:T(8,128)(2,1)S(1)} %merge.1.near_ref, bf16[8,5,24,128]{3,2,1,0:T(8,128)(2,1)S(1)} %collective-permute-done.4.far_ref, bf16[768,4096]{1,0:T(8,128)(2,1)S(1)} %get-tuple-element.33.refs_0_, ...), custom_call_target="tpu_custom_call" | custom-call | flops 6039797760 | bytes 75497472 | tf_op jit(solution)/shard_map/experts/pallas_call | solution.py:333
  40.1 0.7 %collective-permute-start.5 = (bf16[8,5,24,128]{3,2,1,0:T(8,128)(2,1)}, bf16[8,5,24,128]{3,2,1,0:T(8,128)(2,1)S(1)}, u32[]{:S(2)}, u32[]{:S(2)}) collective-permute-start(bf16[8,5,24,128]{3,2,1,0:T(8,128)(2,1)} %get-tuple-element.36), channel_id=1, source_target_pairs={{0,1},{1,0},{2,3},{3,2},{4,5},{5,4},{6,7},{7,6},{8,9},{9,8},{10,11... | collective-permute-start | bytes 737288 | tf_op jit(solution)/shard_map/ppermute | solution.py:44
  40.8 1.3 %collective-permute-done.5.other_ref = bf16[8,5,24,128]{3,2,1,0:T(8,128)(2,1)S(1)} collective-permute-done((bf16[8,5,24,128]{3,2,1,0:T(8,128)(2,1)}, bf16[8,5,24,128]{3,2,1,0:T(8,128)(2,1)S(1)}, u32[]{:S(2)}, u32[]{:S(2)}) %collective-permute-start.5) | collective-permute-done | bytes 245792 | tf_op jit(solution)/shard_map/ppermute | solution.py:44
  42.1 0.0 copy-start
  42.1 1.0 %copy-done = f32[8,5,24,128]{3,2,1,0:T(8,128)S(1)} copy-done((f32[8,5,24,128]{3,2,1,0:T(8,128)S(1)}, f32[8,5,24,128]{3,2,1,0:T(8,128)}, u32[]{:S(2)}) %copy-start) | copy-done | bytes 491544
  43.2 0.8 %add.10 = (bf16[8,5,24,128]{3,2,1,0:T(8,128)(2,1)}, f32[8,128]{1,0:T(8,128)S(1)}) custom-call(f32[8,5,24,128]{3,2,1,0:T(8,128)S(1)} %copy-done, bf16[8,5,24,128]{3,2,1,0:T(8,128)(2,1)S(1)} %collective-permute-done.5.other_ref), custom_call_target="tpu_custom_call" | custom-call | tf_op jit(solution)/shard_map/add/pallas_call | solution.py:368
  43.9 0.0 collective-permute-done.7.refs_2_
  43.9 0.4 collective-permute-done.6.refs_1_
  44.3 0.8 %collective-permute-start.8 = (bf16[2,256,512]{2,1,0:T(8,128)(2,1)S(1)}, bf16[2,256,512]{2,1,0:T(8,128)(2,1)S(1)}, u32[]{:S(2)}, u32[]{:S(2)}) collective-permute-start(bf16[2,256,512]{2,1,0:T(8,128)(2,1)S(1)} %get-tuple-element.39.b0), channel_id=1, source_target_pairs={{0,1},{1,0},{2,3},{3,2},{4,5},{5,4},{6,7},{7,6},{8,9},{9,8},{10,11... | collective-permute-start | bytes 1572872 | tf_op jit(solution)/shard_map/ppermute | solution.py:44
  45.2 0.0 collective-permute-start.9
  45.2 0.5 collective-permute-start.10
  45.7 6.2 %all-to-all-start = ((bf16[8,5,24,128]{3,2,1,0:T(8,128)(2,1)}), bf16[8,5,24,128]{3,2,1,0:T(8,128)(2,1)S(1)}, u32[]{:S(2)}, u32[]{:S(2)}) async-start(bf16[8,5,24,128]{3,2,1,0:T(8,128)(2,1)} %get-tuple-element.42), calls=%async_computation | async-start | bytes 491520 | tf_op jit(solution)/shard_map/all_to_all | solution.py:55
  51.9 0.0 copy-done.2
  51.9 0.0 copy-done.3
  52.0 0.1 pad_add_fusion.place_ref
  52.0 0.0 collective-permute-done.8.b3
  52.0 0.0 collective-permute-done.9.b4
  52.0 0.0 collective-permute-done.10.b5
  52.1 0.0 copy-done.1
  52.1 11.1 %attention.1 = bf16[256,3072]{1,0:T(8,128)(2,1)} custom-call(s32[6]{0:T(128)S(1)} %pad_add_fusion.place_ref, s32[2,6]{1,0:T(2,128)S(1)} %copy-done.1, bf16[256,3072]{1,0:T(8,128)(2,1)} %query_ref.1, bf16[2,256,512]{2,1,0:T(8,128)(2,1)S(1)} %get-tuple-element.39.b0, bf16[2,256,512]{2,1,0:T(8,128)(2,1)S(1)} %get-tuple-element.40.b1, ...), custom_call_target="tpu_custom_call" | custom-call | flops 2415919104 | bytes 6291456 | tf_op jit(solution)/shard_map/attention/pallas_call | solution.py:534
  63.2 0.0 all-to-all-done.back_ref
  63.2 1.5 %combine.1 = bf16[16,3072]{1,0:T(8,128)(2,1)} custom-call(s32[2,16]{1,0:T(2,128)} %bitcast.7, f32[2,16]{1,0:T(2,128)S(1)} %get-tuple-element.44.shares_ref, bf16[8,5,24,128]{3,2,1,0:T(8,128)(2,1)S(1)} %all-to-all-done.back_ref), custom_call_target="tpu_custom_call" | custom-call | tf_op jit(solution)/shard_map/combine/pallas_call | solution.py:421
  (5 shorter events, 0.0 us)
Async XLA Ops:
  1.8 4.3 %collective-permute-start = (bf16[4,5,24,128]{3,2,1,0:T(8,128)(2,1)S(1)}, bf16[4,5,24,128]{3,2,1,0:T(8,128)(2,1)S(1)}, u32[]{:S(2)}, u32[]{:S(2)}) collective-permute-start(bf16[4,5,24,128]{3,2,1,0:T(8,128)(2,1)S(1)} %get-tuple-element.25), channel_id=1, source_target_pairs={{0,2},{1,3},{2,0},{3,1},{4,6},{5,7},{6,4},{7,5},{8,10},{9,11},{10,... | collective-permute-start | bytes 368648 | tf_op jit(solution)/shard_map/ppermute | solution.py:44
  6.0 10.1 %collective-permute-start.1 = (bf16[2,5,24,128]{3,2,1,0:T(8,128)(2,1)S(1)}, bf16[2,5,24,128]{3,2,1,0:T(8,128)(2,1)S(1)}, u32[]{:S(2)}, u32[]{:S(2)}) collective-permute-start(bf16[2,5,24,128]{3,2,1,0:T(8,128)(2,1)S(1)} %get-tuple-element.30), channel_id=1, source_target_pairs={{0,4},{1,5},{2,6},{3,7},{4,0},{5,1},{6,2},{7,3},{8,12},{9,13},{10,... | collective-permute-start | bytes 184328 | tf_op jit(solution)/shard_map/ppermute | solution.py:44
  6.3 9.8 %collective-permute-start.2 = (bf16[2,5,24,128]{3,2,1,0:T(8,128)(2,1)S(1)}, bf16[2,5,24,128]{3,2,1,0:T(8,128)(2,1)S(1)}, u32[]{:S(2)}, u32[]{:S(2)}) collective-permute-start(bf16[2,5,24,128]{3,2,1,0:T(8,128)(2,1)S(1)} %get-tuple-element.31), channel_id=1, source_target_pairs={{0,8},{1,9},{2,10},{3,11},{4,12},{5,13},{6,14},{7,15},{8,0},{9,1},... | collective-permute-start | bytes 184328 | tf_op jit(solution)/shard_map/ppermute | solution.py:44
  8.6 7.6 %collective-permute-start.3 = (bf16[2,5,24,128]{3,2,1,0:T(8,128)(2,1)S(1)}, bf16[2,5,24,128]{3,2,1,0:T(8,128)(2,1)S(1)}, u32[]{:S(2)}, u32[]{:S(2)}) collective-permute-start(bf16[2,5,24,128]{3,2,1,0:T(8,128)(2,1)S(1)} %get-tuple-element.32), channel_id=1, source_target_pairs={{0,12},{1,13},{2,14},{3,15},{4,8},{5,9},{6,10},{7,11},{8,4},{9,5},... | collective-permute-start | bytes 184328 | tf_op jit(solution)/shard_map/ppermute | solution.py:44
  16.2 5.0 %collective-permute-start.4 = (bf16[8,5,24,128]{3,2,1,0:T(8,128)(2,1)S(1)}, bf16[8,5,24,128]{3,2,1,0:T(8,128)(2,1)S(1)}, u32[]{:S(2)}, u32[]{:S(2)}) collective-permute-start(bf16[8,5,24,128]{3,2,1,0:T(8,128)(2,1)S(1)} %merge.1.near_ref), channel_id=1, source_target_pairs={{0,1},{1,0},{2,3},{3,2},{4,5},{5,4},{6,7},{7,6},{8,9},{9,8},{10,11... | collective-permute-start | bytes 737288 | tf_op jit(solution)/shard_map/ppermute | solution.py:44
  18.7 25.2 %collective-permute-start.7 = (bf16[2,256,512]{2,1,0:T(8,128)(2,1)S(1)}, bf16[2,256,512]{2,1,0:T(8,128)(2,1)S(1)}, u32[]{:S(2)}, u32[]{:S(2)}) collective-permute-start(bf16[2,256,512]{2,1,0:T(8,128)(2,1)S(1)} %get-tuple-element.38.refs_0_), channel_id=1, source_target_pairs={{0,4},{1,5},{2,6},{3,7},{4,8},{5,9},{6,10},{7,11},{8,12},{9,13},{1... | collective-permute-start | bytes 1572872 | tf_op jit(solution)/shard_map/ppermute | solution.py:49
  20.0 24.4 %collective-permute-start.6 = (bf16[2,256,512]{2,1,0:T(8,128)(2,1)S(1)}, bf16[2,256,512]{2,1,0:T(8,128)(2,1)S(1)}, u32[]{:S(2)}, u32[]{:S(2)}) collective-permute-start(bf16[2,256,512]{2,1,0:T(8,128)(2,1)S(1)} %get-tuple-element.38.refs_0_), channel_id=1, source_target_pairs={{0,2},{1,3},{2,4},{3,5},{4,6},{5,7},{6,8},{7,9},{8,10},{9,11},{10,... | collective-permute-start | bytes 1572872 | tf_op jit(solution)/shard_map/ppermute | solution.py:49
  21.2 30.7 %copy-start.2 = (s32[5]{0:T(128)S(1)}, s32[5]{0:T(128)}, u32[]{:S(2)}) copy-start(s32[5]{0:T(128)} %constant.39.clone) | copy-start | bytes 64
  21.2 30.7 %copy-start.3 = (s32[5]{0:T(128)S(1)}, s32[5]{0:T(128)}, u32[]{:S(2)}) copy-start(s32[5]{0:T(128)} %constant.38.clone) | copy-start | bytes 64
  21.2 30.9 %copy-start.1 = (s32[2,6]{1,0:T(2,128)S(1)}, s32[2,6]{1,0:T(2,128)}, u32[]{:S(2)}) copy-start(s32[2,6]{1,0:T(2,128)} %lists_ref.1) | copy-start | bytes 148
  40.1 2.0 %collective-permute-start.5 = (bf16[8,5,24,128]{3,2,1,0:T(8,128)(2,1)}, bf16[8,5,24,128]{3,2,1,0:T(8,128)(2,1)S(1)}, u32[]{:S(2)}, u32[]{:S(2)}) collective-permute-start(bf16[8,5,24,128]{3,2,1,0:T(8,128)(2,1)} %get-tuple-element.36), channel_id=1, source_target_pairs={{0,1},{1,0},{2,3},{3,2},{4,5},{5,4},{6,7},{7,6},{8,9},{9,8},{10,11... | collective-permute-start | bytes 737288 | tf_op jit(solution)/shard_map/ppermute | solution.py:44
  42.1 1.0 %copy-start = (f32[8,5,24,128]{3,2,1,0:T(8,128)S(1)}, f32[8,5,24,128]{3,2,1,0:T(8,128)}, u32[]{:S(2)}) copy-start(f32[8,5,24,128]{3,2,1,0:T(8,128)} %get-tuple-element.35.mine_ref) | copy-start | bytes 1474564
  44.3 7.7 %collective-permute-start.8 = (bf16[2,256,512]{2,1,0:T(8,128)(2,1)S(1)}, bf16[2,256,512]{2,1,0:T(8,128)(2,1)S(1)}, u32[]{:S(2)}, u32[]{:S(2)}) collective-permute-start(bf16[2,256,512]{2,1,0:T(8,128)(2,1)S(1)} %get-tuple-element.39.b0), channel_id=1, source_target_pairs={{0,1},{1,0},{2,3},{3,2},{4,5},{5,4},{6,7},{7,6},{8,9},{9,8},{10,11... | collective-permute-start | bytes 1572872 | tf_op jit(solution)/shard_map/ppermute | solution.py:44
  45.2 6.9 %collective-permute-start.9 = (bf16[2,256,512]{2,1,0:T(8,128)(2,1)S(1)}, bf16[2,256,512]{2,1,0:T(8,128)(2,1)S(1)}, u32[]{:S(2)}, u32[]{:S(2)}) collective-permute-start(bf16[2,256,512]{2,1,0:T(8,128)(2,1)S(1)} %get-tuple-element.40.b1), channel_id=1, source_target_pairs={{0,1},{1,0},{2,3},{3,2},{4,5},{5,4},{6,7},{7,6},{8,9},{9,8},{10,11... | collective-permute-start | bytes 1572872 | tf_op jit(solution)/shard_map/ppermute | solution.py:44
  45.2 6.9 %collective-permute-start.10 = (bf16[2,256,512]{2,1,0:T(8,128)(2,1)S(1)}, bf16[2,256,512]{2,1,0:T(8,128)(2,1)S(1)}, u32[]{:S(2)}, u32[]{:S(2)}) collective-permute-start(bf16[2,256,512]{2,1,0:T(8,128)(2,1)S(1)} %get-tuple-element.41.b2), channel_id=1, source_target_pairs={{0,1},{1,0},{2,3},{3,2},{4,5},{5,4},{6,7},{7,6},{8,9},{9,8},{10,11... | collective-permute-start | bytes 1572872 | tf_op jit(solution)/shard_map/ppermute | solution.py:44
  45.7 17.5 %all-to-all-start = ((bf16[8,5,24,128]{3,2,1,0:T(8,128)(2,1)}), bf16[8,5,24,128]{3,2,1,0:T(8,128)(2,1)S(1)}, u32[]{:S(2)}, u32[]{:S(2)}) async-start(bf16[8,5,24,128]{3,2,1,0:T(8,128)(2,1)} %get-tuple-element.42), calls=%async_computation | async-start | bytes 491520 | tf_op jit(solution)/shard_map/all_to_all | solution.py:55
where the time goes:
time: 65.1 us; the launch traced here: 64.7 us
  Pallas kernels  43.7 us (67%)
  starting transfers between devices  17.2 us (26%)
  waiting for transfers between devices  1.9 us (3%)
  local copies, waits for them, and re-layouts  1.04 us (2%)
  between operations  0.77 us (1%)
    pallas_call x1, Pallas kernels, experts(): pl.pallas_call(functools.partial(experts_kernel, len(gate_held)), out_sha...  18.9 us
    pallas_call x1, Pallas kernels, attention(): pl.pallas_call(attention_kernel, out_shape=jax.ShapeDtypeStruct(queries.s...  11.1 us
    ppermute x9, starting transfers between devices, exchanged(): return lax.ppermute(x, 'ctx', [(i, i ^ by) for i in range(devices)])  8.49 us
    pallas_call x1, Pallas kernels, prepare(): pl.pallas_call(functools.partial(prepare_kernel, first), out_shape=(jax.S...  7.41 us
    all_to_all x1, starting transfers between devices, same_core_exchange(): lax.all_to_all(x, 'ctx', split_axis=0, concat_axis=0, tiled=True, axis_in...  6.24 us
    pallas_call x1, Pallas kernels, hold(): pl.pallas_call(functools.partial(hold_kernel, first), out_shape=(jax.Shap...  2.87 us
    ppermute x2, starting transfers between devices, passed_along(): lax.ppermute(x, 'ctx', [(i, (i + by) % devices) for i in range(devices)])  2.51 us
    pallas_call x1, Pallas kernels, combine(): pl.pallas_call(combine_kernel, out_shape=jax.ShapeDtypeStruct((tokens, D)...  1.49 us
  transfers between devices with their start and end apart: 12, of which 3 were waited for; matrix products, arithmetic and copies ran while one was open for 0% of the time, Pallas kernels for 63%

commit v1 on v0

--- a/solution.py
+++ b/solution.py
@@ -22,11 +22,14 @@
 PARTS = 24
 PART_WIDTH = D // PARTS
 PIECES = 4
-FIRST_HELD = D // 4
+HELD_ROWS = (768, 768)
+STREAMED_FROM = sum(HELD_ROWS)
 HIDDEN_CHUNK = 512
-HEADS_PER_STEP = 2
+HEADS_PER_STEP = 4
 LOG2_E = 1.4426950408889634
 MIB = 2**20
+
+SMALL_COST = pl.CostEstimate(flops=10**6, bytes_accessed=10**5, transcendentals=0)
 
 WINDOW_SOURCES = ((2, 5, 1, 4, 0), (2, 4, 1, 3, 0))
 
@@ -53,6 +56,16 @@
     devices = lax.axis_size("ctx")
     groups = [[core + 2 * i for i in range(devices // 2)] for core in range(2)]
     return lax.all_to_all(x, "ctx", split_axis=0, concat_axis=0, tiled=True, axis_index_groups=groups)
+
+
+def row_copies(source, first, target, sems):
+    rows = target.shape[0] // PIECES
+    return [
+        pltpu.make_async_copy(
+            source.at[pl.ds(first + piece * rows, rows)], target.at[pl.ds(piece * rows, rows)], sems.at[piece]
+        )
+        for piece in range(PIECES)
+    ]
 
 
 def pack_kernel(ids_ref, base_ref, tokens_ref, keep_ref, send_ref, rows_ref, slots_ref, count_ref):
@@ -85,7 +98,7 @@
         pack_kernel,
         out_shape=(jax.ShapeDtypeStruct(half, jnp.bfloat16),) * 2,
         in_specs=[smem, smem, vmem],
-        out_specs=(vmem, vmem),
+        out_specs=(vmem,) * 2,
         scratch_shapes=[
             pltpu.VMEM((tokens * PARTS, PART_WIDTH), jnp.float32),
             pltpu.VMEM((2,) + half, jnp.bfloat16),
@@ -135,13 +148,7 @@
 
 
 def hold_kernel(first, mark_ref, gate_ref, next_ref, held_ref, sems):
-    rows = held_ref.shape[0] // PIECES
-    copies = [
-        pltpu.make_async_copy(
-            gate_ref.at[pl.ds(first + piece * rows, rows)], held_ref.at[pl.ds(piece * rows, rows)], sems.at[piece]
-        )
-        for piece in range(PIECES)
-    ]
+    copies = row_copies(gate_ref, first, held_ref, sems)
     for copy in copies:
         copy.start()
     next_ref[...] = mark_ref[...] + 1
@@ -185,17 +192,10 @@
     first, mark_ref, ids_ref, tokens_ref, router_ref, gate_ref, key_ref, value_ref,
     next_ref, shares_ref, pair_ref, held_ref, tokens_vmem, router_vmem, sems, pair_sems,
 ):
-    rows = held_ref.shape[0] // PIECES
     copies = [
         pltpu.make_async_copy(ref, pair_ref.at[place], pair_sems.at[place])
         for place, ref in enumerate((key_ref, value_ref))
-    ]
-    copies += [
-        pltpu.make_async_copy(
-            gate_ref.at[pl.ds(first + piece * rows, rows)], held_ref.at[pl.ds(piece * rows, rows)], sems.at[piece]
-        )
-        for piece in range(PIECES)
-    ]
+    ] + row_copies(gate_ref, first, held_ref, sems)
     small = [
         pltpu.make_async_copy(tokens_ref, tokens_vmem, pair_sems.at[2]),
         pltpu.make_async_copy(router_ref, router_vmem, pair_sems.at[3]),
@@ -238,7 +238,7 @@
 
 def experts_kernel(helds, base_ref, near_ref, far_ref, *refs):
     gate_refs, refs = refs[:helds], refs[helds:]
-    up_ref, down_ref, mine_ref, other_ref, parts_ref, rows_ref, sums_ref, up_vmem, down_vmem, sems = refs
+    gate_ref, up_ref, down_ref, mine_ref, other_ref, parts_ref, rows_ref, sums_ref, gate_vmem, up_vmem, down_vmem, sems = refs
     senders = mine_ref.shape[0]
     count = 2 * senders * CAP
     chunks = up_ref.shape[1] // HIDDEN_CHUNK
@@ -247,6 +247,10 @@
     def span(chunk):
         return pl.ds(pl.multiple_of(chunk * HIDDEN_CHUNK, HIDDEN_CHUNK), HIDDEN_CHUNK)
 
+    def gate_copy(chunk, slot):
+        rest = pl.ds(STREAMED_FROM, D - STREAMED_FROM)
+        return pltpu.make_async_copy(gate_ref.at[rest, span(chunk)], gate_vmem.at[slot], sems.at[2, slot])
+
     def up_copy(chunk, slot):
         return pltpu.make_async_copy(up_ref.at[:, span(chunk)], up_vmem.at[slot], sems.at[0, slot])
 
@@ -254,6 +258,7 @@
         return pltpu.make_async_copy(down_ref.at[span(chunk)], down_vmem.at[slot], sems.at[1, slot])
 
     for chunk in range(min(depth, chunks)):
+        gate_copy(chunk, chunk).start()
         up_copy(chunk, chunk).start()
         down_copy(chunk, chunk).start()
     for place, ref in enumerate((near_ref, far_ref)):
@@ -280,12 +285,15 @@
             )
             gate_value = part if gate_value is None else gate_value + part
             first_row += ref.shape[0]
+        gate_copy(chunk, slot).wait()
+        gate_value += jnp.dot(rows_ref[:, STREAMED_FROM:], gate_vmem[slot], preferred_element_type=jnp.float32)
         up_copy(chunk, slot).wait()
         up_value = jnp.dot(rows_ref[...], up_vmem[slot], preferred_element_type=jnp.float32)
         hidden = (gate_value / (1.0 + jnp.exp(-gate_value)) * up_value).astype(jnp.bfloat16)
 
         @pl.when(chunk + depth < chunks)
         def _():
+            gate_copy(chunk + depth, slot).start()
             up_copy(chunk + depth, slot).start()
 
         down_copy(chunk, slot).wait()
@@ -323,7 +331,7 @@
     lax.fori_loop(0, senders, give, 0)
 
 
-def experts(base, near, far, gate_held, up_weight, down_weight):
+def experts(base, near, far, gate_held, gate_weight, up_weight, down_weight):
     shape = near.shape
     count = 2 * shape[0] * CAP
     smem = pl.BlockSpec(memory_space=pltpu.SMEM)
@@ -332,27 +340,27 @@
     depth = min(3, up_weight.shape[1] // HIDDEN_CHUNK)
     return pl.pallas_call(
         functools.partial(experts_kernel, len(gate_held)),
-        out_shape=(jax.ShapeDtypeStruct(shape, jnp.float32), jax.ShapeDtypeStruct(shape, jnp.bfloat16)),
-        in_specs=[smem] + [vmem] * (2 + len(gate_held)) + [anywhere, anywhere],
+        out_shape=(pltpu.VMEM(shape, jnp.float32), pltpu.VMEM(shape, jnp.bfloat16)),
+        in_specs=[smem] + [vmem] * (2 + len(gate_held)) + [anywhere] * 3,
         out_specs=(vmem, vmem),
         scratch_shapes=[
             pltpu.VMEM((count * PARTS, PART_WIDTH), jnp.float32),
             pltpu.VMEM((count, D), jnp.bfloat16),
             pltpu.VMEM((count, D), jnp.float32),
+            pltpu.VMEM((depth, D - STREAMED_FROM, HIDDEN_CHUNK), jnp.bfloat16),
             pltpu.VMEM((depth, D, HIDDEN_CHUNK), jnp.bfloat16),
             pltpu.VMEM((depth, HIDDEN_CHUNK, D), jnp.bfloat16),
-            pltpu.SemaphoreType.DMA((2, depth)),
+            pltpu.SemaphoreType.DMA((3, depth)),
         ],
         compiler_params=pltpu.CompilerParams(vmem_limit_bytes=32 * MIB),
-        cost_estimate=pl.CostEstimate(
-            flops=6 * count * up_weight.size, bytes_accessed=6 * up_weight.size, transcendentals=0
-        ),
+        cost_estimate=SMALL_COST,
         name="experts",
     )(
         base,
         in_vmem(near),
         in_vmem(far),
         *map(in_vmem, gate_held),
+        in_hbm(gate_weight),
         in_hbm(up_weight),
         in_hbm(down_weight),
     )
@@ -392,7 +400,8 @@
     )(mark, *arrays)
 
 
-def combine_kernel(ids_ref, shares_ref, back_ref, out_ref, rows_ref, count_ref):
+def combine_kernel(ids_ref, shares_ref, back_ref, attended_ref, out_ref, rows_ref, count_ref):
+    del attended_ref
     tokens = out_ref.shape[0]
     holders = back_ref.shape[0] // EXPERTS
     for expert in range(EXPERTS):
@@ -414,14 +423,14 @@
         out_ref[:, columns] = rows_ref[pl.ds(part, tokens, stride=PARTS), :].astype(jnp.bfloat16)
 
 
-def combine(ids, gate_shares, back):
+def combine(ids, gate_shares, back, attended):
     tokens = ids.shape[1]
     smem = pl.BlockSpec(memory_space=pltpu.SMEM)
     vmem = pl.BlockSpec(memory_space=pltpu.VMEM)
     return pl.pallas_call(
         combine_kernel,
         out_shape=jax.ShapeDtypeStruct((tokens, D), jnp.bfloat16),
-        in_specs=[smem, smem, vmem],
+        in_specs=[smem, smem, vmem, pl.BlockSpec(memory_space=pl.ANY)],
         out_specs=vmem,
         scratch_shapes=[
             pltpu.VMEM((tokens * PARTS, PART_WIDTH), jnp.float32),
@@ -429,38 +438,59 @@
         ],
         compiler_params=pltpu.CompilerParams(vmem_limit_bytes=16 * MIB),
         name="combine",
-    )(in_hbm(ids), gate_shares, back)
+    )(in_hbm(ids), gate_shares, back, in_hbm(attended))
 
 
 def attention_kernel(
-    place_ref, lists_ref, query_ref, b0, b1, b2, b3, b4, b5, out_ref, window, scores, weights, sems
+    place_ref, lists_ref, query_ref, b0, b1, b2, b3, b4, b5, out_ref, staged, scores, weights, done, sems
 ):
-    tile, step = pl.program_id(0), pl.program_id(1)
-    copies = [
-        pltpu.make_async_copy(ref, window.at[i], sems.at[i]) for i, ref in enumerate((b0, b1, b2, b3, b4, b5))
-    ]
-
-    @pl.when((tile == 0) & (step == 0))
-    def _():
-        for copy in copies:
-            copy.start()
-        for copy in copies:
-            copy.wait()
-
-    tiles_here = b0.shape[1] // TILE_POSITIONS
-    first_tile = place_ref[0]
-    listed_count = jnp.int32(1)
-    for entry in range(1, MOST_LISTED):
-        listed_count += (lists_ref[tile, entry] >= 0).astype(jnp.int32)
-
-    def fetch(which, entry, head):
-        relative = jnp.clip(lists_ref[tile, entry] - first_tile, 0, (PRIOR_DEVICES + 1) * tiles_here - 1)
-        source = place_ref[1 + lax.div(relative, tiles_here)]
-        first = pl.multiple_of(lax.rem(relative, tiles_here) * TILE_POSITIONS, TILE_POSITIONS)
-        columns = pl.ds(pl.multiple_of((step * HEADS_PER_STEP + head) * HEAD_SIZE, HEAD_SIZE), HEAD_SIZE)
-        return window[source, which, pl.ds(first, TILE_POSITIONS), columns]
-
-    def attend(listed):
+    blocks = (b0, b1, b2, b3, b4, b5)
+    tiles_here = query_ref.shape[0] // TILE_POSITIONS
+    steps = KEY_VALUE_HEADS // HEADS_PER_STEP
+    step_width = HEADS_PER_STEP * QUERY_PER_GROUP * HEAD_SIZE
+    rounds = tiles_here * steps
+
+    def out_copy(turn, slot):
+        rows = pl.ds(pl.multiple_of(lax.div(turn, steps) * TILE_POSITIONS, TILE_POSITIONS), TILE_POSITIONS)
+        columns = pl.ds(pl.multiple_of(lax.rem(turn, steps) * step_width, step_width), step_width)
+        return pltpu.make_async_copy(done.at[slot], out_ref.at[rows, columns], sems.at[slot])
+
+    def gather(tile, count):
+        def one(entry):
+            relative = jnp.clip(lists_ref[tile, entry] - place_ref[0], 0, (PRIOR_DEVICES + 1) * tiles_here - 1)
+            source = place_ref[1 + lax.div(relative, tiles_here)]
+            first = pl.multiple_of(lax.rem(relative, tiles_here) * TILE_POSITIONS, TILE_POSITIONS)
+            for number, block in enumerate(blocks):
+
+                @pl.when(source == number)
+                def _(block=block):
+                    for which in range(2):
+                        staged[which, entry * TILE_POSITIONS : (entry + 1) * TILE_POSITIONS, :] = block[
+                            which, pl.ds(first, TILE_POSITIONS), :
+                        ]
+
+        for entry in range(MOST_LISTED):
+            pl.when(entry < count)(functools.partial(one, entry))
+
+    def turn_body(turn, carry):
+        tile, step = lax.div(turn, steps), lax.rem(turn, steps)
+        slot = lax.rem(turn, 2)
+        count = jnp.int32(1)
+        for entry in range(1, MOST_LISTED):
+            count += (lists_ref[tile, entry] >= 0).astype(jnp.int32)
+        pl.when(step == 0)(functools.partial(gather, tile, count))
+
+        @pl.when(turn >= 2)
+        def _():
+            out_copy(turn - 2, slot).wait()
+
+        for listed in range(1, MOST_LISTED + 1):
+            pl.when(count == listed)(functools.partial(attend, tile, step, slot, listed))
+        out_copy(turn, slot).start()
+        return carry
+
+    def attend(tile, step, slot, listed):
+        query_rows = pl.ds(pl.multiple_of(tile * TILE_POSITIONS, TILE_POSITIONS), TILE_POSITIONS)
         width = listed * TILE_POSITIONS
         units = [(head, part) for head in range(HEADS_PER_STEP) for part in range(2)]
         group_count = QUERY_PER_GROUP // 2
@@ -469,15 +499,20 @@
         causal = column_place <= row_place
         totals = {}
 
-        def columns_of(unit, group):
+        def first_column(unit, group):
             head, part = units[unit]
-            first = (head * QUERY_PER_GROUP + part * group_count + group) * HEAD_SIZE
-            return slice(first, first + HEAD_SIZE)
+            return (head * QUERY_PER_GROUP + part * group_count + group) * HEAD_SIZE
+
+        def query(unit, group):
+            first = pl.multiple_of(step * step_width + first_column(unit, group), HEAD_SIZE)
+            return query_ref[query_rows, pl.ds(first, HEAD_SIZE)]
+
+        def head_columns(unit):
+            return pl.ds(pl.multiple_of((step * HEADS_PER_STEP + units[unit][0]) * HEAD_SIZE, HEAD_SIZE), HEAD_SIZE)
 
         def score(unit):
-            head = units[unit][0]
-            rows = jnp.concatenate([query_ref[:, columns_of(unit, group)] for group in range(group_count)], axis=0)
-            keys = jnp.concatenate([fetch(0, entry, head) for entry in range(listed)], axis=0)
+            rows = jnp.concatenate([query(unit, group) for group in range(group_count)], axis=0)
+            keys = staged[0, :width, head_columns(unit)]
             scores[unit, :, :width] = lax.dot_general(
                 rows, keys, (((1,), (1,)), ((), ())), preferred_element_type=jnp.float32
             )
@@ -501,15 +536,15 @@
                     weights[unit, rows, entry * TILE_POSITIONS : (entry + 1) * TILE_POSITIONS] = weight.astype(
                         jnp.bfloat16
                     )
-                totals[unit, group] = jnp.sum(total, axis=1, keepdims=True)
+                totals[unit, group] = 1.0 / jnp.sum(total, axis=1, keepdims=True)
 
         def finish(unit):
-            head = units[unit][0]
-            values = jnp.concatenate([fetch(1, entry, head) for entry in range(listed)], axis=0)
+            values = staged[1, :width, head_columns(unit)]
             summed = jnp.dot(weights[unit, :, :width], values, preferred_element_type=jnp.float32)
             for group in range(group_count):
                 rows = slice(group * TILE_POSITIONS, (group + 1) * TILE_POSITIONS)
-                out_ref[:, columns_of(unit, group)] = (summed[rows] / totals[unit, group]).astype(jnp.bfloat16)
+                first = first_column(unit, group)
+                done[slot, :, first : first + HEAD_SIZE] = (summed[rows] * totals[unit, group]).astype(jnp.bfloat16)
 
         for turn in range(len(units) + 2):
             if turn < len(units):
@@ -519,39 +554,31 @@
             if 0 <= turn - 1 < len(units):
                 weigh(turn - 1)
 
-    for listed in range(1, MOST_LISTED + 1):
-        pl.when(listed_count == listed)(functools.partial(attend, listed))
+    lax.fori_loop(0, rounds, turn_body, 0)
+    for turn in range(max(rounds - 2, 0), rounds):
+        out_copy(jnp.int32(turn), turn % 2).wait()
 
 
 def attention(place, tile_lists, queries, blocks):
-    rows_here = queries.shape[0]
-    tiles_here = rows_here // TILE_POSITIONS
-    group_width = HEADS_PER_STEP * QUERY_PER_GROUP * HEAD_SIZE
-    anywhere = pl.BlockSpec(memory_space=pl.ANY)
-    query_spec = pl.BlockSpec((TILE_POSITIONS, group_width), lambda tile, step, *_: (tile, step))
+    smem = pl.BlockSpec(memory_space=pltpu.SMEM)
+    vmem = pl.BlockSpec(memory_space=pltpu.VMEM)
     unit = (2 * HEADS_PER_STEP, QUERY_PER_GROUP // 2 * TILE_POSITIONS, MOST_LISTED * TILE_POSITIONS)
-    most = MOST_LISTED * TILE_POSITIONS
     return pl.pallas_call(
         attention_kernel,
         out_shape=jax.ShapeDtypeStruct(queries.shape, jnp.bfloat16),
-        grid_spec=pltpu.PrefetchScalarGridSpec(
-            num_scalar_prefetch=2,
-            grid=(tiles_here, KEY_VALUE_HEADS // HEADS_PER_STEP),
-            in_specs=[query_spec] + [anywhere] * 6,
-            out_specs=query_spec,
-            scratch_shapes=[
-                pltpu.VMEM((6, 2, rows_here, KEY_VALUE_HEADS * HEAD_SIZE), jnp.bfloat16),
-                pltpu.VMEM(unit, jnp.float32),
-                pltpu.VMEM(unit, jnp.bfloat16),
-                pltpu.SemaphoreType.DMA((6,)),
-            ],
-        ),
-        compiler_params=pltpu.CompilerParams(vmem_limit_bytes=24 * MIB),
-        cost_estimate=pl.CostEstimate(
-            flops=4 * most * queries.size, bytes_accessed=8 * queries.size, transcendentals=most * queries.size // 128
-        ),
+        in_specs=[smem, smem] + [vmem] * 7,
+        out_specs=pl.BlockSpec(memory_space=pl.ANY),
+        scratch_shapes=[
+            pltpu.VMEM((2, MOST_LISTED * TILE_POSITIONS, KEY_VALUE_HEADS * HEAD_SIZE), jnp.bfloat16),
+            pltpu.VMEM(unit, jnp.float32),
+            pltpu.VMEM(unit, jnp.bfloat16),
+            pltpu.VMEM((2, TILE_POSITIONS, HEADS_PER_STEP * QUERY_PER_GROUP * HEAD_SIZE), jnp.bfloat16),
+            pltpu.SemaphoreType.DMA((2,)),
+        ],
+        compiler_params=pltpu.CompilerParams(vmem_limit_bytes=32 * MIB),
+        cost_estimate=SMALL_COST,
         name="attention",
-    )(place, tile_lists, in_hbm(queries), *blocks)
+    )(place, tile_lists, queries, *blocks)
 
 
 def shards(
@@ -571,26 +598,27 @@
     ids = expert_ids.T
     direct = devices == 2 * EXPERTS
     base = (me // 2 if direct else jnp.zeros_like(me)).astype(jnp.int32)[None]
+    gate_held = []
     keep, send = pack(ids, base, moe_tokens)
     mark = jnp.zeros((8, 128), jnp.float32)
     rest = (ids, moe_tokens, router_weight, gate_weight, key_matrix, value_matrix)
     if direct:
         came = exchanged(send, 2)
-        mark, first_held = hold(mark, gate_weight, 0, FIRST_HELD)
+        mark, held = hold(mark, gate_weight, 0, HELD_ROWS[0])
+        gate_held.append(held)
         *pieces, mark = join(keep, came, mark)
         pieces[1:] = [exchanged(pieces[place], 4 * place) for place in range(1, len(pieces))]
-        mark, gate_shares, own, second_held = prepare(mark, *rest, FIRST_HELD, D - FIRST_HELD)
+        mark, gate_shares, own, held = prepare(mark, *rest, HELD_ROWS[0], HELD_ROWS[1])
         near = merge(mark, pieces)
-        gate_held = [first_held, second_held]
     else:
         packed = jnp.stack([keep, send], axis=1).reshape((EXPERTS,) + keep.shape[1:])
         near = same_core_exchange(jnp.repeat(packed, devices // (2 * EXPERTS), axis=0))
-        mark, gate_shares, own, held = prepare(mark, *rest, 0, D)
-        gate_held = [held]
+        mark, gate_shares, own, held = prepare(mark, *rest, 0, STREAMED_FROM)
+    gate_held.append(held)
     far = exchanged(near, 1)
     two_before = passed_along(own, 2)
     four_before = passed_along(own, 4)
-    mine, other = experts(base, near, far, gate_held, up_weight, down_weight)
+    mine, other = experts(base, near, far, gate_held, gate_weight, up_weight, down_weight)
     summed, mark = add(mine, exchanged(other, 1))
     back = same_core_exchange(summed)
     blocks = list(follow(mark, [own, two_before, four_before]))
@@ -599,8 +627,7 @@
     sources = jnp.where(me % 2 == 0, *(jnp.array(row, jnp.int32) for row in WINDOW_SOURCES))
     place = jnp.concatenate([((me - PRIOR_DEVICES) * tiles_here).astype(jnp.int32)[None], sources])
     attended = attention(place, tile_lists, queries, blocks)
-    attended, back = lax.optimization_barrier((attended, back))
-    combined = combine(ids, gate_shares, back)
+    combined = combine(ids, gate_shares, back, attended)
     return (attended, combined)
 
 

time: 65.1 us -> 59.7 us (0.917)
  the two profiles are of different devices: /device:TPU:9 before, /device:TPU:0 now
where the time goes in v1:
time: 59.7 us; the launch traced here: 59 us
  Pallas kernels  35.8 us (60%)
  starting transfers between devices  15.7 us (26%)
  waiting for transfers between devices  6.59 us (11%)
  between operations  0.79 us (1%)
    pallas_call x1, Pallas kernels, experts(): pl.pallas_call(functools.partial(experts_kernel, len(gate_held)), out_sha...  20.6 us
    ppermute x9, starting transfers between devices, exchanged(): return lax.ppermute(x, 'ctx', [(i, i ^ by) for i in range(devices)])  8.46 us
    pallas_call x1, Pallas kernels, attention(): pl.pallas_call(attention_kernel, out_shape=jax.ShapeDtypeStruct(queries.s...  5.81 us
    all_to_all x1, starting transfers between devices, same_core_exchange(): lax.all_to_all(x, 'ctx', split_axis=0, concat_axis=0, tiled=True, axis_in...  4.78 us
    pallas_call x1, Pallas kernels, prepare(): pl.pallas_call(functools.partial(prepare_kernel, first), out_shape=(jax.S...  3.8 us
    ppermute x9, waiting for transfers between devices, exchanged(): return lax.ppermute(x, 'ctx', [(i, i ^ by) for i in range(devices)])  3.34 us
    all_to_all x1, waiting for transfers between devices, same_core_exchange(): lax.all_to_all(x, 'ctx', split_axis=0, concat_axis=0, tiled=True, axis_in...  3.25 us
    pallas_call x1, Pallas kernels, hold(): pl.pallas_call(functools.partial(hold_kernel, first), out_shape=(jax.Shap...  2.87 us
  transfers between devices with their start and end apart: 12, of which 4 were waited for; matrix products, arithmetic and copies ran while one was open for 0% of the time, Pallas kernels for 56%

profile of v1, /device:TPU:0, one launch (start us, length us, event | category | flops | bytes accessed | tf_op | source)
XLA Modules:
  0.0 59.0 jit_solution(10917707238113743118)
XLA Ops:
  0.6 1.1 %pack.1 = (bf16[4,5,24,128]{3,2,1,0:T(8,128)(2,1)S(1)}, bf16[4,5,24,128]{3,2,1,0:T(8,128)(2,1)S(1)}) custom-call(s32[2,16]{1,0:T(2,128)} %bitcast.5, s32[1]{0:T(128)} %bitcast.1.base_ref, bf16[16,3072]{1,0:T(8,128)(2,1)} %tokens_ref.3), custom_call_target="tpu_custom_call" | custom-call | tf_op jit(solution)/shard_map/pack/pallas_call | solution.py:97
  1.8 3.0 %collective-permute-start = (bf16[4,5,24,128]{3,2,1,0:T(8,128)(2,1)S(1)}, bf16[4,5,24,128]{3,2,1,0:T(8,128)(2,1)S(1)}, u32[]{:S(2)}, u32[]{:S(2)}) collective-permute-start(bf16[4,5,24,128]{3,2,1,0:T(8,128)(2,1)S(1)} %get-tuple-element.23), channel_id=1, source_target_pairs={{0,2},{1,3},{2,0},{3,1},{4,6},{5,7},{6,4},{7,5},{8,10},{9,11},{10,... | collective-permute-start | bytes 368648 | tf_op jit(solution)/shard_map/ppermute | solution.py:47
  4.8 2.9 %hold.1 = (f32[8,128]{1,0:T(8,128)S(1)}, bf16[768,4096]{1,0:T(8,128)(2,1)S(1)}) custom-call(f32[8,128]{1,0:T(8,128)S(1)} %broadcast_in_dim.11.mark_ref, bf16[3072,4096]{1,0:T(8,128)(2,1)} %refs_2_.1), custom_call_target="tpu_custom_call" | custom-call | flops 1000000 | bytes 6291456 | tf_op jit(solution)/shard_map/hold/pallas_call | solution.py:163
  7.6 0.4 collective-permute-done.came_ref
  8.1 1.9 %collective-permute-start.1 = (bf16[2,5,24,128]{3,2,1,0:T(8,128)(2,1)S(1)}, bf16[2,5,24,128]{3,2,1,0:T(8,128)(2,1)S(1)}, u32[]{:S(2)}, u32[]{:S(2)}) collective-permute-start(bf16[2,5,24,128]{3,2,1,0:T(8,128)(2,1)S(1)} %get-tuple-element.28), channel_id=1, source_target_pairs={{0,4},{1,5},{2,6},{3,7},{4,0},{5,1},{6,2},{7,3},{8,12},{9,13},{10,... | collective-permute-start | bytes 184328 | tf_op jit(solution)/shard_map/ppermute | solution.py:47
  10.0 2.6 %collective-permute-start.2 = (bf16[2,5,24,128]{3,2,1,0:T(8,128)(2,1)S(1)}, bf16[2,5,24,128]{3,2,1,0:T(8,128)(2,1)S(1)}, u32[]{:S(2)}, u32[]{:S(2)}) collective-permute-start(bf16[2,5,24,128]{3,2,1,0:T(8,128)(2,1)S(1)} %get-tuple-element.29), channel_id=1, source_target_pairs={{0,8},{1,9},{2,10},{3,11},{4,12},{5,13},{6,14},{7,15},{8,0},{9,1},... | collective-permute-start | bytes 184328 | tf_op jit(solution)/shard_map/ppermute | solution.py:47
  12.6 0.0 collective-permute-start.3
  12.6 3.8 %prepare.1 = (f32[8,128]{1,0:T(8,128)S(1)}, f32[2,16]{1,0:T(2,128)S(1)}, bf16[2,256,512]{2,1,0:T(8,128)(2,1)S(1)}, bf16[768,4096]{1,0:T(8,128)(2,1)S(1)}) custom-call(f32[8,128]{1,0:T(8,128)S(1)} %get-tuple-element.25.mark_ref, s32[2,16]{1,0:T(2,128)} %bitcast.6, bf16[16,3072]{1,0:T(8,128)(2,1)} %tokens_ref.3, bf16[8,3072]{1,0:T(8,128)(2,1)} %bitcast.4, ...), custom_call_target="tpu_custom_call" | custom-call | flops 1000000 | bytes 6291456 | tf_op jit(solution)/shard_map/prepare/pallas_call | solution.py:217
  16.4 0.9 %collective-permute-start.7 = (bf16[2,256,512]{2,1,0:T(8,128)(2,1)S(1)}, bf16[2,256,512]{2,1,0:T(8,128)(2,1)S(1)}, u32[]{:S(2)}, u32[]{:S(2)}) collective-permute-start(bf16[2,256,512]{2,1,0:T(8,128)(2,1)S(1)} %get-tuple-element.36.refs_0_), channel_id=1, source_target_pairs={{0,4},{1,5},{2,6},{3,7},{4,8},{5,9},{6,10},{7,11},{8,12},{9,13},{1... | collective-permute-start | bytes 1572872 | tf_op jit(solution)/shard_map/ppermute | solution.py:52
  17.3 1.5 %collective-permute-start.6 = (bf16[2,256,512]{2,1,0:T(8,128)(2,1)S(1)}, bf16[2,256,512]{2,1,0:T(8,128)(2,1)S(1)}, u32[]{:S(2)}, u32[]{:S(2)}) collective-permute-start(bf16[2,256,512]{2,1,0:T(8,128)(2,1)S(1)} %get-tuple-element.36.refs_0_), channel_id=1, source_target_pairs={{0,2},{1,3},{2,4},{3,5},{4,6},{5,7},{6,8},{7,9},{8,10},{9,11},{10,... | collective-permute-start | bytes 1572872 | tf_op jit(solution)/shard_map/ppermute | solution.py:52
  18.8 0.0 collective-permute-done.1.refs_1_
  18.8 0.0 collective-permute-done.2.refs_2_
  18.8 0.0 collective-permute-done.3.refs_3_
  18.9 0.1 collective-permute-start.4
  19.0 1.5 %collective-permute-done.4.far_ref = bf16[8,5,24,128]{3,2,1,0:T(8,128)(2,1)S(1)} collective-permute-done((bf16[8,5,24,128]{3,2,1,0:T(8,128)(2,1)S(1)}, bf16[8,5,24,128]{3,2,1,0:T(8,128)(2,1)S(1)}, u32[]{:S(2)}, u32[]{:S(2)}) %collective-permute-start.4) | collective-permute-done | bytes 245792 | tf_op jit(solution)/shard_map/ppermute | solution.py:47
  20.5 0.0 copy-start.3
  20.5 0.0 copy-start.4
  20.5 0.0 copy-start
  20.5 0.0 copy-start.2
  20.5 20.6 %experts.1 = (f32[8,5,24,128]{3,2,1,0:T(8,128)S(1)}, bf16[8,5,24,128]{3,2,1,0:T(8,128)(2,1)S(1)}) custom-call(s32[1]{0:T(128)} %bitcast.1.base_ref, bf16[8,5,24,128]{3,2,1,0:T(8,128)(2,1)S(1)} %merge.1.near_ref, bf16[8,5,24,128]{3,2,1,0:T(8,128)(2,1)S(1)} %collective-permute-done.4.far_ref, bf16[768,4096]{1,0:T(8,128)(2,1)S(1)} %get-tuple-element.31.refs_0_, ...), custom_call_target="tpu_custom_call" | custom-call | flops 1000000 | bytes 100000 | tf_op jit(solution)/shard_map/experts/pallas_call | solution.py:341
  41.1 0.2 collective-permute-start.5
  41.3 1.4 %collective-permute-done.5.other_ref = bf16[8,5,24,128]{3,2,1,0:T(8,128)(2,1)S(1)} collective-permute-done((bf16[8,5,24,128]{3,2,1,0:T(8,128)(2,1)S(1)}, bf16[8,5,24,128]{3,2,1,0:T(8,128)(2,1)S(1)}, u32[]{:S(2)}, u32[]{:S(2)}) %collective-permute-start.5) | collective-permute-done | bytes 245792 | tf_op jit(solution)/shard_map/ppermute | solution.py:47
  42.7 0.1 add.10
  42.7 0.0 copy-start.1
  42.7 0.0 collective-permute-done.7.refs_2_
  42.8 0.0 collective-permute-done.6.refs_1_
  42.8 0.2 collective-permute-start.8
  43.0 0.4 collective-permute-start.9
  43.4 0.1 collective-permute-start.10
  43.5 0.0 copy-done.1
  43.5 4.8 %all-to-all-start = ((bf16[8,5,24,128]{3,2,1,0:T(8,128)(2,1)}), bf16[8,5,24,128]{3,2,1,0:T(8,128)(2,1)S(1)}, u32[]{:S(2)}, u32[]{:S(2)}) async-start(bf16[8,5,24,128]{3,2,1,0:T(8,128)(2,1)} %copy-done.1), calls=%async_computation | async-start | bytes 491520 | tf_op jit(solution)/shard_map/all_to_all | solution.py:58
  48.3 0.0 copy-done.3
  48.3 0.0 copy-done.4
  48.3 0.1 pad_add_fusion.place_ref
  48.4 0.0 collective-permute-done.8.b3
  48.4 0.0 collective-permute-done.9.b4
  48.4 0.0 collective-permute-done.10.b5
  48.4 0.0 copy-done
  48.4 0.0 copy-done.2
  48.4 5.8 %attention.1.attended_ref = bf16[256,3072]{1,0:T(8,128)(2,1)} custom-call(s32[6]{0:T(128)S(1)} %pad_add_fusion.place_ref, s32[2,6]{1,0:T(2,128)S(1)} %copy-done.2, bf16[256,3072]{1,0:T(8,128)(2,1)S(1)} %copy-done, bf16[2,256,512]{2,1,0:T(8,128)(2,1)S(1)} %get-tuple-element.37.b0, bf16[2,256,512]{2,1,0:T(8,128)(2,1)S(1)} %get-tuple-element.38.b1, ...), custom_call_target="tpu_custom_call" | custom-call | flops 1000000 | bytes 100000 | tf_op jit(solution)/shard_map/attention/pallas_call | solution.py:566
  54.2 3.2 %all-to-all-done.back_ref = bf16[8,5,24,128]{3,2,1,0:T(8,128)(2,1)S(1)} async-done(((bf16[8,5,24,128]{3,2,1,0:T(8,128)(2,1)}), bf16[8,5,24,128]{3,2,1,0:T(8,128)(2,1)S(1)}, u32[]{:S(2)}, u32[]{:S(2)}) %all-to-all-start) | async-done | bytes 245792 | tf_op jit(solution)/shard_map/all_to_all | solution.py:58
  57.5 1.5 %combine.1 = bf16[16,3072]{1,0:T(8,128)(2,1)} custom-call(s32[2,16]{1,0:T(2,128)} %bitcast.7, f32[2,16]{1,0:T(2,128)S(1)} %get-tuple-element.40.shares_ref, bf16[8,5,24,128]{3,2,1,0:T(8,128)(2,1)S(1)} %all-to-all-done.back_ref, bf16[256,3072]{1,0:T(8,128)(2,1)} %attention.1.attended_ref), custom_call_target="tpu_custom_call" | custom-call | tf_op jit(solution)/shard_map/combine/pallas_call | solution.py:430
  (5 shorter events, 0.0 us)
Async XLA Ops:
  1.8 6.3 %collective-permute-start = (bf16[4,5,24,128]{3,2,1,0:T(8,128)(2,1)S(1)}, bf16[4,5,24,128]{3,2,1,0:T(8,128)(2,1)S(1)}, u32[]{:S(2)}, u32[]{:S(2)}) collective-permute-start(bf16[4,5,24,128]{3,2,1,0:T(8,128)(2,1)S(1)} %get-tuple-element.23), channel_id=1, source_target_pairs={{0,2},{1,3},{2,0},{3,1},{4,6},{5,7},{6,4},{7,5},{8,10},{9,11},{10,... | collective-permute-start | bytes 368648 | tf_op jit(solution)/shard_map/ppermute | solution.py:47
  8.1 10.7 %collective-permute-start.1 = (bf16[2,5,24,128]{3,2,1,0:T(8,128)(2,1)S(1)}, bf16[2,5,24,128]{3,2,1,0:T(8,128)(2,1)S(1)}, u32[]{:S(2)}, u32[]{:S(2)}) collective-permute-start(bf16[2,5,24,128]{3,2,1,0:T(8,128)(2,1)S(1)} %get-tuple-element.28), channel_id=1, source_target_pairs={{0,4},{1,5},{2,6},{3,7},{4,0},{5,1},{6,2},{7,3},{8,12},{9,13},{10,... | collective-permute-start | bytes 184328 | tf_op jit(solution)/shard_map/ppermute | solution.py:47
  10.0 8.8 %collective-permute-start.2 = (bf16[2,5,24,128]{3,2,1,0:T(8,128)(2,1)S(1)}, bf16[2,5,24,128]{3,2,1,0:T(8,128)(2,1)S(1)}, u32[]{:S(2)}, u32[]{:S(2)}) collective-permute-start(bf16[2,5,24,128]{3,2,1,0:T(8,128)(2,1)S(1)} %get-tuple-element.29), channel_id=1, source_target_pairs={{0,8},{1,9},{2,10},{3,11},{4,12},{5,13},{6,14},{7,15},{8,0},{9,1},... | collective-permute-start | bytes 184328 | tf_op jit(solution)/shard_map/ppermute | solution.py:47
  12.6 6.3 %collective-permute-start.3 = (bf16[2,5,24,128]{3,2,1,0:T(8,128)(2,1)S(1)}, bf16[2,5,24,128]{3,2,1,0:T(8,128)(2,1)S(1)}, u32[]{:S(2)}, u32[]{:S(2)}) collective-permute-start(bf16[2,5,24,128]{3,2,1,0:T(8,128)(2,1)S(1)} %get-tuple-element.30), channel_id=1, source_target_pairs={{0,12},{1,13},{2,14},{3,15},{4,8},{5,9},{6,10},{7,11},{8,4},{9,5},... | collective-permute-start | bytes 184328 | tf_op jit(solution)/shard_map/ppermute | solution.py:47
  16.4 26.4 %collective-permute-start.7 = (bf16[2,256,512]{2,1,0:T(8,128)(2,1)S(1)}, bf16[2,256,512]{2,1,0:T(8,128)(2,1)S(1)}, u32[]{:S(2)}, u32[]{:S(2)}) collective-permute-start(bf16[2,256,512]{2,1,0:T(8,128)(2,1)S(1)} %get-tuple-element.36.refs_0_), channel_id=1, source_target_pairs={{0,4},{1,5},{2,6},{3,7},{4,8},{5,9},{6,10},{7,11},{8,12},{9,13},{1... | collective-permute-start | bytes 1572872 | tf_op jit(solution)/shard_map/ppermute | solution.py:52
  17.3 25.4 %collective-permute-start.6 = (bf16[2,256,512]{2,1,0:T(8,128)(2,1)S(1)}, bf16[2,256,512]{2,1,0:T(8,128)(2,1)S(1)}, u32[]{:S(2)}, u32[]{:S(2)}) collective-permute-start(bf16[2,256,512]{2,1,0:T(8,128)(2,1)S(1)} %get-tuple-element.36.refs_0_), channel_id=1, source_target_pairs={{0,2},{1,3},{2,4},{3,5},{4,6},{5,7},{6,8},{7,9},{8,10},{9,11},{10,... | collective-permute-start | bytes 1572872 | tf_op jit(solution)/shard_map/ppermute | solution.py:52
  18.9 1.6 %collective-permute-start.4 = (bf16[8,5,24,128]{3,2,1,0:T(8,128)(2,1)S(1)}, bf16[8,5,24,128]{3,2,1,0:T(8,128)(2,1)S(1)}, u32[]{:S(2)}, u32[]{:S(2)}) collective-permute-start(bf16[8,5,24,128]{3,2,1,0:T(8,128)(2,1)S(1)} %merge.1.near_ref), channel_id=1, source_target_pairs={{0,1},{1,0},{2,3},{3,2},{4,5},{5,4},{6,7},{7,6},{8,9},{9,8},{10,11... | collective-permute-start | bytes 737288 | tf_op jit(solution)/shard_map/ppermute | solution.py:47
  20.5 27.8 %copy-start.3 = (s32[5]{0:T(128)S(1)}, s32[5]{0:T(128)}, u32[]{:S(2)}) copy-start(s32[5]{0:T(128)} %constant.39.clone) | copy-start | bytes 64
  20.5 27.8 %copy-start.4 = (s32[5]{0:T(128)S(1)}, s32[5]{0:T(128)}, u32[]{:S(2)}) copy-start(s32[5]{0:T(128)} %constant.38.clone) | copy-start | bytes 64
  20.5 27.9 %copy-start = (bf16[256,3072]{1,0:T(8,128)(2,1)S(1)}, bf16[256,3072]{1,0:T(8,128)(2,1)}, u32[]{:S(2)}) copy-start(bf16[256,3072]{1,0:T(8,128)(2,1)} %query_ref.1) | copy-start | bytes 4718596
  20.5 27.9 %copy-start.2 = (s32[2,6]{1,0:T(2,128)S(1)}, s32[2,6]{1,0:T(2,128)}, u32[]{:S(2)}) copy-start(s32[2,6]{1,0:T(2,128)} %lists_ref.1) | copy-start | bytes 148
  41.1 1.6 %collective-permute-start.5 = (bf16[8,5,24,128]{3,2,1,0:T(8,128)(2,1)S(1)}, bf16[8,5,24,128]{3,2,1,0:T(8,128)(2,1)S(1)}, u32[]{:S(2)}, u32[]{:S(2)}) collective-permute-start(bf16[8,5,24,128]{3,2,1,0:T(8,128)(2,1)S(1)} %get-tuple-element.34), channel_id=1, source_target_pairs={{0,1},{1,0},{2,3},{3,2},{4,5},{5,4},{6,7},{7,6},{8,9},{9,8},{10,11... | collective-permute-start | bytes 737288 | tf_op jit(solution)/shard_map/ppermute | solution.py:47
  42.7 0.8 %copy-start.1 = (bf16[8,5,24,128]{3,2,1,0:T(8,128)(2,1)}, bf16[8,5,24,128]{3,2,1,0:T(8,128)(2,1)S(1)}, u32[]{:S(2)}) copy-start(bf16[8,5,24,128]{3,2,1,0:T(8,128)(2,1)S(1)} %get-tuple-element.41) | copy-start | bytes 737284
  42.8 5.6 %collective-permute-start.8 = (bf16[2,256,512]{2,1,0:T(8,128)(2,1)S(1)}, bf16[2,256,512]{2,1,0:T(8,128)(2,1)}, u32[]{:S(2)}, u32[]{:S(2)}) collective-permute-start(bf16[2,256,512]{2,1,0:T(8,128)(2,1)S(1)} %get-tuple-element.37.b0), channel_id=1, source_target_pairs={{0,1},{1,0},{2,3},{3,2},{4,5},{5,4},{6,7},{7,6},{8,9},{9,8},{10,11... | collective-permute-start | bytes 1572872 | tf_op jit(solution)/shard_map/ppermute | solution.py:47
  43.0 5.4 %collective-permute-start.9 = (bf16[2,256,512]{2,1,0:T(8,128)(2,1)S(1)}, bf16[2,256,512]{2,1,0:T(8,128)(2,1)}, u32[]{:S(2)}, u32[]{:S(2)}) collective-permute-start(bf16[2,256,512]{2,1,0:T(8,128)(2,1)S(1)} %get-tuple-element.38.b1), channel_id=1, source_target_pairs={{0,1},{1,0},{2,3},{3,2},{4,5},{5,4},{6,7},{7,6},{8,9},{9,8},{10,11... | collective-permute-start | bytes 1572872 | tf_op jit(solution)/shard_map/ppermute | solution.py:47
  43.4 5.0 %collective-permute-start.10 = (bf16[2,256,512]{2,1,0:T(8,128)(2,1)S(1)}, bf16[2,256,512]{2,1,0:T(8,128)(2,1)}, u32[]{:S(2)}, u32[]{:S(2)}) collective-permute-start(bf16[2,256,512]{2,1,0:T(8,128)(2,1)S(1)} %get-tuple-element.39.b2), channel_id=1, source_target_pairs={{0,1},{1,0},{2,3},{3,2},{4,5},{5,4},{6,7},{7,6},{8,9},{9,8},{10,11... | collective-permute-start | bytes 1572872 | tf_op jit(solution)/shard_map/ppermute | solution.py:47
  43.5 14.0 %all-to-all-start = ((bf16[8,5,24,128]{3,2,1,0:T(8,128)(2,1)}), bf16[8,5,24,128]{3,2,1,0:T(8,128)(2,1)S(1)}, u32[]{:S(2)}, u32[]{:S(2)}) async-start(bf16[8,5,24,128]{3,2,1,0:T(8,128)(2,1)} %copy-done.1), calls=%async_computation | async-start | bytes 491520 | tf_op jit(solution)/shard_map/all_to_all | solution.py:58

commit v2 on v1

--- a/solution.py
+++ b/solution.py
@@ -21,7 +21,7 @@
 
 PARTS = 24
 PART_WIDTH = D // PARTS
-PIECES = 4
+PIECES = 16
 HELD_ROWS = (768, 768)
 STREAMED_FROM = sum(HELD_ROWS)
 HIDDEN_CHUNK = 512
@@ -438,7 +438,7 @@
         ],
         compiler_params=pltpu.CompilerParams(vmem_limit_bytes=16 * MIB),
         name="combine",
-    )(in_hbm(ids), gate_shares, back, in_hbm(attended))
+    )(ids, gate_shares, back, in_hbm(attended))
 
 
 def attention_kernel(
@@ -450,10 +450,16 @@
     step_width = HEADS_PER_STEP * QUERY_PER_GROUP * HEAD_SIZE
     rounds = tiles_here * steps
 
-    def out_copy(turn, slot):
+    head_width = QUERY_PER_GROUP * HEAD_SIZE
+
+    def out_copy(turn, slot, head):
         rows = pl.ds(pl.multiple_of(lax.div(turn, steps) * TILE_POSITIONS, TILE_POSITIONS), TILE_POSITIONS)
-        columns = pl.ds(pl.multiple_of(lax.rem(turn, steps) * step_width, step_width), step_width)
-        return pltpu.make_async_copy(done.at[slot], out_ref.at[rows, columns], sems.at[slot])
+        first = lax.rem(turn, steps) * step_width + head * head_width
+        return pltpu.make_async_copy(
+            done.at[slot, :, pl.ds(head * head_width, head_width)],
+            out_ref.at[rows, pl.ds(pl.multiple_of(first, head_width), head_width)],
+            sems.at[slot, head],
+        )
 
     def gather(tile, count):
         def one(entry):
@@ -482,14 +488,15 @@
 
         @pl.when(turn >= 2)
         def _():
-            out_copy(turn - 2, slot).wait()
+            for head in range(HEADS_PER_STEP):
+                out_copy(turn - 2, slot, head).wait()
 
         for listed in range(1, MOST_LISTED + 1):
-            pl.when(count == listed)(functools.partial(attend, tile, step, slot, listed))
-        out_copy(turn, slot).start()
+            pl.when(count == listed)(functools.partial(attend, turn, slot, listed))
         return carry
 
-    def attend(tile, step, slot, listed):
+    def attend(turn, slot, listed):
+        tile, step = lax.div(turn, steps), lax.rem(turn, steps)
         query_rows = pl.ds(pl.multiple_of(tile * TILE_POSITIONS, TILE_POSITIONS), TILE_POSITIONS)
         width = listed * TILE_POSITIONS
         units = [(head, part) for head in range(HEADS_PER_STEP) for part in range(2)]
@@ -546,17 +553,20 @@
                 first = first_column(unit, group)
                 done[slot, :, first : first + HEAD_SIZE] = (summed[rows] * totals[unit, group]).astype(jnp.bfloat16)
 
-        for turn in range(len(units) + 2):
-            if turn < len(units):
-                score(turn)
-            if 0 <= turn - 2:
-                finish(turn - 2)
-            if 0 <= turn - 1 < len(units):
-                weigh(turn - 1)
+        for stage in range(len(units) + 2):
+            if stage < len(units):
+                score(stage)
+            if 0 <= stage - 2:
+                finish(stage - 2)
+                if units[stage - 2][1] == 1:
+                    out_copy(turn, slot, units[stage - 2][0]).start()
+            if 0 <= stage - 1 < len(units):
+                weigh(stage - 1)
 
     lax.fori_loop(0, rounds, turn_body, 0)
     for turn in range(max(rounds - 2, 0), rounds):
-        out_copy(jnp.int32(turn), turn % 2).wait()
+        for head in range(HEADS_PER_STEP):
+            out_copy(jnp.int32(turn), turn % 2, head).wait()
 
 
 def attention(place, tile_lists, queries, blocks):
@@ -573,7 +583,7 @@
             pltpu.VMEM(unit, jnp.float32),
             pltpu.VMEM(unit, jnp.bfloat16),
             pltpu.VMEM((2, TILE_POSITIONS, HEADS_PER_STEP * QUERY_PER_GROUP * HEAD_SIZE), jnp.bfloat16),
-            pltpu.SemaphoreType.DMA((2,)),
+            pltpu.SemaphoreType.DMA((2, HEADS_PER_STEP)),
         ],
         compiler_params=pltpu.CompilerParams(vmem_limit_bytes=32 * MIB),
         cost_estimate=SMALL_COST,

time: 59.7 us -> 59.4 us (level)
  no operation moved by 1% of the time
where the time goes in v2:
time: 59.4 us; the launch traced here: 58.9 us
  Pallas kernels  35.6 us (60%)
  starting transfers between devices  15.7 us (26%)
  waiting for transfers between devices  6.72 us (11%)
  between operations  0.8 us (1%)
    pallas_call x1, Pallas kernels, experts(): pl.pallas_call(functools.partial(experts_kernel, len(gate_held)), out_sha...  20.6 us
    ppermute x9, starting transfers between devices, exchanged(): return lax.ppermute(x, 'ctx', [(i, i ^ by) for i in range(devices)])  8.46 us
    pallas_call x1, Pallas kernels, attention(): pl.pallas_call(attention_kernel, out_shape=jax.ShapeDtypeStruct(queries.s...  5.64 us
    all_to_all x1, starting transfers between devices, same_core_exchange(): lax.all_to_all(x, 'ctx', split_axis=0, concat_axis=0, tiled=True, axis_in...  4.77 us
    pallas_call x1, Pallas kernels, prepare(): pl.pallas_call(functools.partial(prepare_kernel, first), out_shape=(jax.S...  3.81 us
    all_to_all x1, waiting for transfers between devices, same_core_exchange(): lax.all_to_all(x, 'ctx', split_axis=0, concat_axis=0, tiled=True, axis_in...  3.41 us
    ppermute x9, waiting for transfers between devices, exchanged(): return lax.ppermute(x, 'ctx', [(i, i ^ by) for i in range(devices)])  3.31 us
    pallas_call x1, Pallas kernels, hold(): pl.pallas_call(functools.partial(hold_kernel, first), out_shape=(jax.Shap...  2.91 us
  transfers between devices with their start and end apart: 12, of which 4 were waited for; matrix products, arithmetic and copies ran while one was open for 0% of the time, Pallas kernels for 56%

profile of v2, /device:TPU:0, one launch (start us, length us, event | category | flops | bytes accessed | tf_op | source)
XLA Modules:
  0.0 58.9 jit_solution(9280932899838348878)
XLA Ops:
  0.6 1.1 %pack.1 = (bf16[4,5,24,128]{3,2,1,0:T(8,128)(2,1)S(1)}, bf16[4,5,24,128]{3,2,1,0:T(8,128)(2,1)S(1)}) custom-call(s32[2,16]{1,0:T(2,128)} %bitcast.4, s32[1]{0:T(128)} %bitcast.1.base_ref, bf16[16,3072]{1,0:T(8,128)(2,1)} %tokens_ref.3), custom_call_target="tpu_custom_call" | custom-call | tf_op jit(solution)/shard_map/pack/pallas_call | solution.py:97
  1.8 3.0 %collective-permute-start = (bf16[4,5,24,128]{3,2,1,0:T(8,128)(2,1)S(1)}, bf16[4,5,24,128]{3,2,1,0:T(8,128)(2,1)S(1)}, u32[]{:S(2)}, u32[]{:S(2)}) collective-permute-start(bf16[4,5,24,128]{3,2,1,0:T(8,128)(2,1)S(1)} %get-tuple-element.23), channel_id=1, source_target_pairs={{0,2},{1,3},{2,0},{3,1},{4,6},{5,7},{6,4},{7,5},{8,10},{9,11},{10,... | collective-permute-start | bytes 368648 | tf_op jit(solution)/shard_map/ppermute | solution.py:47
  4.8 2.9 %hold.1 = (f32[8,128]{1,0:T(8,128)S(1)}, bf16[768,4096]{1,0:T(8,128)(2,1)S(1)}) custom-call(f32[8,128]{1,0:T(8,128)S(1)} %broadcast_in_dim.11.mark_ref, bf16[3072,4096]{1,0:T(8,128)(2,1)} %refs_2_.1), custom_call_target="tpu_custom_call" | custom-call | flops 1000000 | bytes 6291456 | tf_op jit(solution)/shard_map/hold/pallas_call | solution.py:163
  7.7 0.4 collective-permute-done.came_ref
  8.1 1.9 %collective-permute-start.1 = (bf16[2,5,24,128]{3,2,1,0:T(8,128)(2,1)S(1)}, bf16[2,5,24,128]{3,2,1,0:T(8,128)(2,1)S(1)}, u32[]{:S(2)}, u32[]{:S(2)}) collective-permute-start(bf16[2,5,24,128]{3,2,1,0:T(8,128)(2,1)S(1)} %get-tuple-element.28), channel_id=1, source_target_pairs={{0,4},{1,5},{2,6},{3,7},{4,0},{5,1},{6,2},{7,3},{8,12},{9,13},{10,... | collective-permute-start | bytes 184328 | tf_op jit(solution)/shard_map/ppermute | solution.py:47
  10.0 2.6 %collective-permute-start.2 = (bf16[2,5,24,128]{3,2,1,0:T(8,128)(2,1)S(1)}, bf16[2,5,24,128]{3,2,1,0:T(8,128)(2,1)S(1)}, u32[]{:S(2)}, u32[]{:S(2)}) collective-permute-start(bf16[2,5,24,128]{3,2,1,0:T(8,128)(2,1)S(1)} %get-tuple-element.29), channel_id=1, source_target_pairs={{0,8},{1,9},{2,10},{3,11},{4,12},{5,13},{6,14},{7,15},{8,0},{9,1},... | collective-permute-start | bytes 184328 | tf_op jit(solution)/shard_map/ppermute | solution.py:47
  12.6 0.0 collective-permute-start.3
  12.6 3.8 %prepare.1 = (f32[8,128]{1,0:T(8,128)S(1)}, f32[2,16]{1,0:T(2,128)S(1)}, bf16[2,256,512]{2,1,0:T(8,128)(2,1)S(1)}, bf16[768,4096]{1,0:T(8,128)(2,1)S(1)}) custom-call(f32[8,128]{1,0:T(8,128)S(1)} %get-tuple-element.25.mark_ref, s32[2,16]{1,0:T(2,128)} %bitcast.5, bf16[16,3072]{1,0:T(8,128)(2,1)} %tokens_ref.3, bf16[8,3072]{1,0:T(8,128)(2,1)} %bitcast.7, ...), custom_call_target="tpu_custom_call" | custom-call | flops 1000000 | bytes 6291456 | tf_op jit(solution)/shard_map/prepare/pallas_call | solution.py:217
  16.4 0.9 %collective-permute-start.7 = (bf16[2,256,512]{2,1,0:T(8,128)(2,1)S(1)}, bf16[2,256,512]{2,1,0:T(8,128)(2,1)S(1)}, u32[]{:S(2)}, u32[]{:S(2)}) collective-permute-start(bf16[2,256,512]{2,1,0:T(8,128)(2,1)S(1)} %get-tuple-element.36.refs_0_), channel_id=1, source_target_pairs={{0,4},{1,5},{2,6},{3,7},{4,8},{5,9},{6,10},{7,11},{8,12},{9,13},{1... | collective-permute-start | bytes 1572872 | tf_op jit(solution)/shard_map/ppermute | solution.py:52
  17.4 1.5 %collective-permute-start.6 = (bf16[2,256,512]{2,1,0:T(8,128)(2,1)S(1)}, bf16[2,256,512]{2,1,0:T(8,128)(2,1)S(1)}, u32[]{:S(2)}, u32[]{:S(2)}) collective-permute-start(bf16[2,256,512]{2,1,0:T(8,128)(2,1)S(1)} %get-tuple-element.36.refs_0_), channel_id=1, source_target_pairs={{0,2},{1,3},{2,4},{3,5},{4,6},{5,7},{6,8},{7,9},{8,10},{9,11},{10,... | collective-permute-start | bytes 1572872 | tf_op jit(solution)/shard_map/ppermute | solution.py:52
  18.9 0.0 collective-permute-done.1.refs_1_
  18.9 0.0 collective-permute-done.2.refs_2_
  18.9 0.0 collective-permute-done.3.refs_3_
  18.9 0.1 collective-permute-start.4
  19.0 1.5 %collective-permute-done.4.far_ref = bf16[8,5,24,128]{3,2,1,0:T(8,128)(2,1)S(1)} collective-permute-done((bf16[8,5,24,128]{3,2,1,0:T(8,128)(2,1)S(1)}, bf16[8,5,24,128]{3,2,1,0:T(8,128)(2,1)S(1)}, u32[]{:S(2)}, u32[]{:S(2)}) %collective-permute-start.4) | collective-permute-done | bytes 245792 | tf_op jit(solution)/shard_map/ppermute | solution.py:47
  20.5 0.0 copy-start.4
  20.5 0.0 copy-start.5
  20.5 0.0 copy-start
  20.5 0.0 copy-start.3
  20.5 20.6 %experts.1 = (f32[8,5,24,128]{3,2,1,0:T(8,128)S(1)}, bf16[8,5,24,128]{3,2,1,0:T(8,128)(2,1)S(1)}) custom-call(s32[1]{0:T(128)} %bitcast.1.base_ref, bf16[8,5,24,128]{3,2,1,0:T(8,128)(2,1)S(1)} %merge.1.near_ref, bf16[8,5,24,128]{3,2,1,0:T(8,128)(2,1)S(1)} %collective-permute-done.4.far_ref, bf16[768,4096]{1,0:T(8,128)(2,1)S(1)} %get-tuple-element.31.refs_0_, ...), custom_call_target="tpu_custom_call" | custom-call | flops 1000000 | bytes 100000 | tf_op jit(solution)/shard_map/experts/pallas_call | solution.py:341
  41.1 0.0 copy-start.2
  41.1 0.2 collective-permute-start.5
  41.3 1.4 %collective-permute-done.5.other_ref = bf16[8,5,24,128]{3,2,1,0:T(8,128)(2,1)S(1)} collective-permute-done((bf16[8,5,24,128]{3,2,1,0:T(8,128)(2,1)S(1)}, bf16[8,5,24,128]{3,2,1,0:T(8,128)(2,1)S(1)}, u32[]{:S(2)}, u32[]{:S(2)}) %collective-permute-start.5) | collective-permute-done | bytes 245792 | tf_op jit(solution)/shard_map/ppermute | solution.py:47
  42.7 0.1 add.10
  42.8 0.0 copy-start.1
  42.8 0.0 collective-permute-done.7.refs_2_
  42.8 0.0 collective-permute-done.6.refs_1_
  42.8 0.2 collective-permute-start.8
  43.0 0.4 collective-permute-start.9
  43.4 0.1 collective-permute-start.10
  43.5 0.0 copy-done.1
  43.5 4.8 %all-to-all-start = ((bf16[8,5,24,128]{3,2,1,0:T(8,128)(2,1)}), bf16[8,5,24,128]{3,2,1,0:T(8,128)(2,1)S(1)}, u32[]{:S(2)}, u32[]{:S(2)}) async-start(bf16[8,5,24,128]{3,2,1,0:T(8,128)(2,1)} %copy-done.1), calls=%async_computation | async-start | bytes 491520 | tf_op jit(solution)/shard_map/all_to_all | solution.py:58
  48.3 0.0 copy-done.4
  48.3 0.0 copy-done.5
  48.3 0.1 pad_add_fusion.place_ref
  48.4 0.0 collective-permute-done.8.b3
  48.4 0.0 collective-permute-done.9.b4
  48.4 0.0 collective-permute-done.10.b5
  48.4 0.0 copy-done
  48.4 0.0 copy-done.3
  48.4 5.6 %attention.1.attended_ref = bf16[256,3072]{1,0:T(8,128)(2,1)} custom-call(s32[6]{0:T(128)S(1)} %pad_add_fusion.place_ref, s32[2,6]{1,0:T(2,128)S(1)} %copy-done.3, bf16[256,3072]{1,0:T(8,128)(2,1)S(1)} %copy-done, bf16[2,256,512]{2,1,0:T(8,128)(2,1)S(1)} %get-tuple-element.37.b0, bf16[2,256,512]{2,1,0:T(8,128)(2,1)S(1)} %get-tuple-element.38.b1, ...), custom_call_target="tpu_custom_call" | custom-call | flops 1000000 | bytes 100000 | tf_op jit(solution)/shard_map/attention/pallas_call | solution.py:576
  54.1 3.4 %all-to-all-done.back_ref = bf16[8,5,24,128]{3,2,1,0:T(8,128)(2,1)S(1)} async-done(((bf16[8,5,24,128]{3,2,1,0:T(8,128)(2,1)}), bf16[8,5,24,128]{3,2,1,0:T(8,128)(2,1)S(1)}, u32[]{:S(2)}, u32[]{:S(2)}) %all-to-all-start) | async-done | bytes 245792 | tf_op jit(solution)/shard_map/all_to_all | solution.py:58
  57.5 0.0 copy-done.2
  57.5 1.4 %combine.1 = bf16[16,3072]{1,0:T(8,128)(2,1)} custom-call(s32[2,16]{1,0:T(2,128)S(1)} %bitcast.6, f32[2,16]{1,0:T(2,128)S(1)} %get-tuple-element.40.shares_ref, bf16[8,5,24,128]{3,2,1,0:T(8,128)(2,1)S(1)} %all-to-all-done.back_ref, bf16[256,3072]{1,0:T(8,128)(2,1)} %attention.1.attended_ref), custom_call_target="tpu_custom_call" | custom-call | tf_op jit(solution)/shard_map/combine/pallas_call | solution.py:430
  (5 shorter events, 0.0 us)
Async XLA Ops:
  1.8 6.3 %collective-permute-start = (bf16[4,5,24,128]{3,2,1,0:T(8,128)(2,1)S(1)}, bf16[4,5,24,128]{3,2,1,0:T(8,128)(2,1)S(1)}, u32[]{:S(2)}, u32[]{:S(2)}) collective-permute-start(bf16[4,5,24,128]{3,2,1,0:T(8,128)(2,1)S(1)} %get-tuple-element.23), channel_id=1, source_target_pairs={{0,2},{1,3},{2,0},{3,1},{4,6},{5,7},{6,4},{7,5},{8,10},{9,11},{10,... | collective-permute-start | bytes 368648 | tf_op jit(solution)/shard_map/ppermute | solution.py:47
  8.1 10.7 %collective-permute-start.1 = (bf16[2,5,24,128]{3,2,1,0:T(8,128)(2,1)S(1)}, bf16[2,5,24,128]{3,2,1,0:T(8,128)(2,1)S(1)}, u32[]{:S(2)}, u32[]{:S(2)}) collective-permute-start(bf16[2,5,24,128]{3,2,1,0:T(8,128)(2,1)S(1)} %get-tuple-element.28), channel_id=1, source_target_pairs={{0,4},{1,5},{2,6},{3,7},{4,0},{5,1},{6,2},{7,3},{8,12},{9,13},{10,... | collective-permute-start | bytes 184328 | tf_op jit(solution)/shard_map/ppermute | solution.py:47
  10.0 8.9 %collective-permute-start.2 = (bf16[2,5,24,128]{3,2,1,0:T(8,128)(2,1)S(1)}, bf16[2,5,24,128]{3,2,1,0:T(8,128)(2,1)S(1)}, u32[]{:S(2)}, u32[]{:S(2)}) collective-permute-start(bf16[2,5,24,128]{3,2,1,0:T(8,128)(2,1)S(1)} %get-tuple-element.29), channel_id=1, source_target_pairs={{0,8},{1,9},{2,10},{3,11},{4,12},{5,13},{6,14},{7,15},{8,0},{9,1},... | collective-permute-start | bytes 184328 | tf_op jit(solution)/shard_map/ppermute | solution.py:47
  12.6 6.3 %collective-permute-start.3 = (bf16[2,5,24,128]{3,2,1,0:T(8,128)(2,1)S(1)}, bf16[2,5,24,128]{3,2,1,0:T(8,128)(2,1)S(1)}, u32[]{:S(2)}, u32[]{:S(2)}) collective-permute-start(bf16[2,5,24,128]{3,2,1,0:T(8,128)(2,1)S(1)} %get-tuple-element.30), channel_id=1, source_target_pairs={{0,12},{1,13},{2,14},{3,15},{4,8},{5,9},{6,10},{7,11},{8,4},{9,5},... | collective-permute-start | bytes 184328 | tf_op jit(solution)/shard_map/ppermute | solution.py:47
  16.4 26.4 %collective-permute-start.7 = (bf16[2,256,512]{2,1,0:T(8,128)(2,1)S(1)}, bf16[2,256,512]{2,1,0:T(8,128)(2,1)S(1)}, u32[]{:S(2)}, u32[]{:S(2)}) collective-permute-start(bf16[2,256,512]{2,1,0:T(8,128)(2,1)S(1)} %get-tuple-element.36.refs_0_), channel_id=1, source_target_pairs={{0,4},{1,5},{2,6},{3,7},{4,8},{5,9},{6,10},{7,11},{8,12},{9,13},{1... | collective-permute-start | bytes 1572872 | tf_op jit(solution)/shard_map/ppermute | solution.py:52
  17.4 25.4 %collective-permute-start.6 = (bf16[2,256,512]{2,1,0:T(8,128)(2,1)S(1)}, bf16[2,256,512]{2,1,0:T(8,128)(2,1)S(1)}, u32[]{:S(2)}, u32[]{:S(2)}) collective-permute-start(bf16[2,256,512]{2,1,0:T(8,128)(2,1)S(1)} %get-tuple-element.36.refs_0_), channel_id=1, source_target_pairs={{0,2},{1,3},{2,4},{3,5},{4,6},{5,7},{6,8},{7,9},{8,10},{9,11},{10,... | collective-permute-start | bytes 1572872 | tf_op jit(solution)/shard_map/ppermute | solution.py:52
  18.9 1.6 %collective-permute-start.4 = (bf16[8,5,24,128]{3,2,1,0:T(8,128)(2,1)S(1)}, bf16[8,5,24,128]{3,2,1,0:T(8,128)(2,1)S(1)}, u32[]{:S(2)}, u32[]{:S(2)}) collective-permute-start(bf16[8,5,24,128]{3,2,1,0:T(8,128)(2,1)S(1)} %merge.1.near_ref), channel_id=1, source_target_pairs={{0,1},{1,0},{2,3},{3,2},{4,5},{5,4},{6,7},{7,6},{8,9},{9,8},{10,11... | collective-permute-start | bytes 737288 | tf_op jit(solution)/shard_map/ppermute | solution.py:47
  20.5 27.8 %copy-start.4 = (s32[5]{0:T(128)S(1)}, s32[5]{0:T(128)}, u32[]{:S(2)}) copy-start(s32[5]{0:T(128)} %constant.39.clone) | copy-start | bytes 64
  20.5 27.8 %copy-start.5 = (s32[5]{0:T(128)S(1)}, s32[5]{0:T(128)}, u32[]{:S(2)}) copy-start(s32[5]{0:T(128)} %constant.38.clone) | copy-start | bytes 64
  20.5 27.9 %copy-start = (bf16[256,3072]{1,0:T(8,128)(2,1)S(1)}, bf16[256,3072]{1,0:T(8,128)(2,1)}, u32[]{:S(2)}) copy-start(bf16[256,3072]{1,0:T(8,128)(2,1)} %query_ref.1) | copy-start | bytes 4718596
  20.5 28.0 %copy-start.3 = (s32[2,6]{1,0:T(2,128)S(1)}, s32[2,6]{1,0:T(2,128)}, u32[]{:S(2)}) copy-start(s32[2,6]{1,0:T(2,128)} %lists_ref.1) | copy-start | bytes 148
  41.1 16.4 %copy-start.2 = (s32[16,2]{0,1:T(2,128)S(1)}, s32[16,2]{0,1:T(2,128)}, u32[]{:S(2)}) copy-start(s32[16,2]{0,1:T(2,128)} %param.17) | copy-start | bytes 388
  41.1 1.6 %collective-permute-start.5 = (bf16[8,5,24,128]{3,2,1,0:T(8,128)(2,1)S(1)}, bf16[8,5,24,128]{3,2,1,0:T(8,128)(2,1)S(1)}, u32[]{:S(2)}, u32[]{:S(2)}) collective-permute-start(bf16[8,5,24,128]{3,2,1,0:T(8,128)(2,1)S(1)} %get-tuple-element.34), channel_id=1, source_target_pairs={{0,1},{1,0},{2,3},{3,2},{4,5},{5,4},{6,7},{7,6},{8,9},{9,8},{10,11... | collective-permute-start | bytes 737288 | tf_op jit(solution)/shard_map/ppermute | solution.py:47
  42.8 0.8 %copy-start.1 = (bf16[8,5,24,128]{3,2,1,0:T(8,128)(2,1)}, bf16[8,5,24,128]{3,2,1,0:T(8,128)(2,1)S(1)}, u32[]{:S(2)}) copy-start(bf16[8,5,24,128]{3,2,1,0:T(8,128)(2,1)S(1)} %get-tuple-element.41) | copy-start | bytes 737284
  42.8 5.6 %collective-permute-start.8 = (bf16[2,256,512]{2,1,0:T(8,128)(2,1)S(1)}, bf16[2,256,512]{2,1,0:T(8,128)(2,1)}, u32[]{:S(2)}, u32[]{:S(2)}) collective-permute-start(bf16[2,256,512]{2,1,0:T(8,128)(2,1)S(1)} %get-tuple-element.37.b0), channel_id=1, source_target_pairs={{0,1},{1,0},{2,3},{3,2},{4,5},{5,4},{6,7},{7,6},{8,9},{9,8},{10,11... | collective-permute-start | bytes 1572872 | tf_op jit(solution)/shard_map/ppermute | solution.py:47
  43.0 5.4 %collective-permute-start.9 = (bf16[2,256,512]{2,1,0:T(8,128)(2,1)S(1)}, bf16[2,256,512]{2,1,0:T(8,128)(2,1)}, u32[]{:S(2)}, u32[]{:S(2)}) collective-permute-start(bf16[2,256,512]{2,1,0:T(8,128)(2,1)S(1)} %get-tuple-element.38.b1), channel_id=1, source_target_pairs={{0,1},{1,0},{2,3},{3,2},{4,5},{5,4},{6,7},{7,6},{8,9},{9,8},{10,11... | collective-permute-start | bytes 1572872 | tf_op jit(solution)/shard_map/ppermute | solution.py:47
  43.4 5.0 %collective-permute-start.10 = (bf16[2,256,512]{2,1,0:T(8,128)(2,1)S(1)}, bf16[2,256,512]{2,1,0:T(8,128)(2,1)}, u32[]{:S(2)}, u32[]{:S(2)}) collective-permute-start(bf16[2,256,512]{2,1,0:T(8,128)(2,1)S(1)} %get-tuple-element.39.b2), channel_id=1, source_target_pairs={{0,1},{1,0},{2,3},{3,2},{4,5},{5,4},{6,7},{7,6},{8,9},{9,8},{10,11... | collective-permute-start | bytes 1572872 | tf_op jit(solution)/shard_map/ppermute | solution.py:47
  43.5 14.0 %all-to-all-start = ((bf16[8,5,24,128]{3,2,1,0:T(8,128)(2,1)}), bf16[8,5,24,128]{3,2,1,0:T(8,128)(2,1)S(1)}, u32[]{:S(2)}, u32[]{:S(2)}) async-start(bf16[8,5,24,128]{3,2,1,0:T(8,128)(2,1)} %copy-done.1), calls=%async_computation | async-start | bytes 491520 | tf_op jit(solution)/shard_map/all_to_all | solution.py:58
